TPU v7x, 32 devices: a whole 2x2x4 slice. The times are simulated.
32 devices in a mesh: tiles: 8 (over z, x), views: 4 (over y, core).
Axes of the slice: x: 2, y: 2, z: 4, core: 2. Of those that a mesh axis runs over, the one named last changes fastest.
Arguments:
- ref_features: bfloat16 [8, 8, 4096], P('tiles'), may hold values from -6 to 6
- partner_lines: bfloat16 [8, 4, 8, 8192], P('tiles'), may hold values from -6 to 6
- line_owner: int32 [8, 32, 1], P('tiles'), may hold values from 0 to 7; in each aligned block of 32 rows (0 to 31, 32 to 63, ..., all dimensions but the last counted through in order) at most 8 rows name the same one
- line_index: int32 [8, 32], P('tiles'), may hold values from 0 to 7
- line_offset: int32 [8, 32], P('tiles'), may hold values from 0 to 64
- neighbours: int32 [8, 4], replicated, may hold values from -1 to 7, as said below
- conv1_weight: bfloat16 [3, 3, 3, 8, 32], replicated, may hold values from -0.4375 to 0.4375
- conv1_bias: float32 [32], replicated, may hold values from -3 to 3
- conv2_weight: bfloat16 [3, 3, 3, 32, 32], replicated, may hold values from -0.21875 to 0.21875
- conv2_bias: float32 [32], replicated, may hold values from -3 to 3
Outputs:
- regularized: float32 [8, 64, 8, 4096], P('tiles', 'views')
Inputs may be any that keep to these rules, and one draw needn't show every extreme that they name: `line_owner`: among the 32 requests of one tile (aligned blocks of rows), no owner is named more than 8 times. Tile positions in a grid of 2 rows and 4 columns are a permutation of the tiles; neighbours lists the tiles above, below, left and right, -1 at the grid's edge.
All inputs are finite; a program needn't handle non-finite values.
Results may differ from a plain program's by a relative error of at most 0.0019.
Values may be sent and summed in bfloat16 or wider, within the bound.
A program may use at most 128 MiB of HBM per device.

v0:
```python
from functools import partial

import jax
import jax.numpy as jnp
from jax import lax
from jax.experimental import pallas as pl
from jax.experimental.pallas import tpu as pltpu
from jax.sharding import PartitionSpec as P

C = 32
G = 8
CH = 32
NDISP = 64
W = 128
SW = 256
NPV = 4
H = 8
LANES = 128
COLS = LANES // C
LROWS = SW // COLS
WROWS = W // COLS
PITCH = WROWS + 16
HX = H + 4
FRONT = 8
LPAD = FRONT + LROWS + 8


def pack_kernel(views, lines_ref, ref_ref, req_ref, out_ref, scr):
    n_lines = lines_ref.shape[0]
    for j in range(LROWS):
        scr[pl.ds(j, n_lines, stride=LROWS), :] = lines_ref[:, j * LANES : (j + 1) * LANES].astype(jnp.float32)
    base = n_lines * LROWS
    for i in range(WROWS):
        scr[pl.ds(base + i, H, stride=WROWS), :] = ref_ref[:, i * LANES : (i + 1) * LANES].astype(jnp.float32)
    base = base + H * WROWS
    rest = scr.shape[0] - base
    scr[base:, :] = jnp.concatenate([req_ref[...], jnp.zeros((rest - req_ref.shape[0], LANES), jnp.float32)], axis=0)
    part = out_ref.shape[0]
    v = lax.axis_index("views")
    out_ref[...] = scr[pl.ds(pl.multiple_of(v * part, 16), part), :].astype(jnp.bfloat16)


def main_kernel(
    n_tiles, nd, req, nb, all_ref, w1, b1, w2, b2, gm, out_ref,
    lines, refb, linef, vt0, vte0, vt, vte, refx, x1, h2, ybuf, sem_l, sem_r,
):
    t = lax.axis_index("tiles")
    v = lax.axis_index("views")
    d0 = v * nd

    def link(x, side):
        got = nb[jnp.maximum(x, 0) * 4 + side]
        return jnp.where(x >= 0, got, -1)

    mids = [t, link(t, 2), link(t, 3)]
    tiles = [[link(m, 0), m, link(m, 1)] for m in mids]
    ref_base = NPV * H * LROWS

    spans = ((0, 2, H - 2), (2, H, 0), (H + 2, 2, 0))
    copies = []
    for s in range(3):
        for band, (at, count, row) in enumerate(spans):
            copies.append(
                pltpu.make_async_copy(
                    all_ref.at[jnp.maximum(tiles[s][band], 0), pl.ds(ref_base + row * WROWS, count * WROWS), :],
                    refb.at[s, pl.ds(at * WROWS, count * WROWS), :],
                    sem_r.at[s * 3 + band],
                )
            )
    for c in copies:
        c.start()

    def tile_of(s, hh):
        return jnp.maximum(
            jnp.where(hh < 2, tiles[s][0], jnp.where(hh < H + 2, tiles[s][1], tiles[s][2])), 0
        )

    def row_of(hh):
        return jnp.where(hh < 2, hh + H - 2, jnp.where(hh < H + 2, hh - 2, hh - H - 2))

    def fetch(hh, carry):
        row = row_of(hh)
        for s in range(3):
            tt = tile_of(s, hh)
            for u in range(NPV):
                j = tt * LANES + u * H + row
                owner = req[j]
                index = req[j + NPV * H]
                src = pl.multiple_of((u * H + index) * LROWS, LROWS)
                pltpu.make_async_copy(
                    all_ref.at[owner, pl.ds(src, LROWS), :], lines.at[s * NPV + u, hh], sem_l
                ).start()
        return carry

    lax.fori_loop(0, HX, fetch, 0)

    for c in copies:
        c.wait()
    edge = lax.broadcasted_iota(jnp.int32, (16, LANES), 0)
    for hh in range(HX):
        band = 0 if hh < 2 else (1 if hh < H + 2 else 2)
        own = refb[0, hh * WROWS : (hh + 1) * WROWS, :].astype(jnp.float32)
        refx[hh, 0:WROWS, :] = jnp.where(tiles[0][band] >= 0, own, 0.0)
        lo = refb[1, (hh + 1) * WROWS - 16 : (hh + 1) * WROWS, :].astype(jnp.float32)
        hi = refb[2, hh * WROWS : hh * WROWS + 16, :].astype(jnp.float32)
        lo = jnp.where(tiles[1][band] >= 0, lo, 0.0)
        hi = jnp.where(tiles[2][band] >= 0, hi, 0.0)
        refx[hh, WROWS:PITCH, :] = jnp.where(edge == 0, hi, jnp.where(edge == 15, lo, 0.0))

    linef[...] = jnp.zeros_like(linef)
    vt0[...] = jnp.zeros_like(vt0)
    vte0[...] = jnp.zeros_like(vte0)
    pltpu.make_async_copy(lines, lines, sem_l).wait()

    lane40 = lax.broadcasted_iota(jnp.int32, (40, LANES), 1)

    def window(buf, first, rows, r0):
        shift = lax.rem(LANES - C * r0, LANES)
        a = pltpu.roll(buf[pl.ds(first, rows), :], shift, 1)
        b = pltpu.roll(buf[pl.ds(first + 1, rows), :], shift, 1)
        return jnp.where(lane40[:rows] < LANES - C * r0, a, b)

    def assemble(hh, carry):
        row = row_of(hh)
        for s in range(3):
            tt = tile_of(s, hh)
            total = None
            for u in range(NPV):
                off = req[tt * LANES + 2 * NPV * H + u * H + row]
                col = off + d0 - 2 + FRONT * COLS
                q = lax.div(col, COLS)
                r0 = col - q * COLS
                slot = s * NPV + u
                buf = linef.at[slot]
                buf[FRONT : FRONT + LROWS, :] = lines[slot, hh].astype(jnp.float32)
                if s == 0:
                    part = window(buf, q, 40, r0)
                elif s == 1:
                    part = window(buf, q + WROWS - 1, 8, r0)
                else:
                    part = window(buf, q, 8, r0)
                total = part if total is None else total + part
            if s == 0:
                vt0[hh, 0:40, :] = total
            else:
                vte0[s - 1, hh, 0:8, :] = total
        return carry

    lax.fori_loop(0, HX, assemble, 0)

    lane1 = lax.broadcasted_iota(jnp.int32, (1, LANES), 1)

    def shift_all(hh, carry):
        for r in range(COLS):
            keep = lane1 < LANES - C * r

            def moved(x, y):
                if r == 0:
                    return x
                s = LANES - C * r
                return jnp.where(keep, pltpu.roll(x, s, 1), pltpu.roll(y, s, 1))

            vt[r, hh] = moved(vt0[hh, 0:40, :], vt0[hh, 1:41, :])
            for side in range(2):
                vte[r, side, hh] = moved(vte0[side, hh, 0:8, :], vte0[side, hh, 1:9, :])
        return carry

    lax.fori_loop(0, HX, shift_all, 0)

    lane_p = lax.broadcasted_iota(jnp.int32, (PITCH, LANES), 1)
    edge3 = lax.broadcasted_iota(jnp.int32, (16, LANES), 0) == 0
    nk = (nd + 4) // COLS
    for k in range(nk):
        def cost_row(hh, carry, k=k):
            parts = []
            ref_rows = refx[hh]
            for r in range(COLS):
                own = vt[r, hh, k : k + WROWS, :]
                side = jnp.where(edge3, vte[r, 1, hh, k : k + 1, :], vte[r, 0, hh, k : k + 1, :])
                prod = ref_rows * jnp.concatenate([own, side], axis=0)
                top = prod.astype(jnp.bfloat16)
                low = (prod - top.astype(jnp.float32)).astype(jnp.bfloat16)
                parts.append(jnp.concatenate([top, low], axis=1))
            cost = jnp.dot(jnp.concatenate(parts, axis=0), gm[...], preferred_element_type=jnp.float32)
            at = pl.multiple_of(hh * PITCH, 16)
            for r in range(COLS):
                c = cost[r * PITCH : (r + 1) * PITCH]
                x = jnp.where(
                    lane_p < COLS * G,
                    c,
                    jnp.where(lane_p < (COLS + 1) * G, pltpu.roll(c, 1, 0), pltpu.roll(c, PITCH - 1, 0)),
                )
                dd = k * COLS + r
                disp = d0 - 2 + dd
                x = jnp.where((disp >= 0) & (disp < NDISP), x, 0.0)
                x1[dd, pl.ds(at, PITCH), :] = x.astype(jnp.bfloat16)
            return carry

        lax.fori_loop(0, HX, cost_row, 0)

    rows1 = (H + 2) * PITCH
    row_id = lax.broadcasted_iota(jnp.int32, (rows1, LANES), 0)
    hrow = row_id // PITCH
    col = row_id - hrow * PITCH

    def inside(s):
        above = jnp.where(tiles[s][0] >= 0, 1, 0)
        mid = jnp.where(tiles[s][1] >= 0, 1, 0)
        below = jnp.where(tiles[s][2] >= 0, 1, 0)
        return jnp.where(hrow == 0, above, jnp.where(hrow == H + 1, below, mid))

    valid = jnp.where(col < WROWS, inside(0), jnp.where(col == WROWS, inside(2), inside(1)))
    lane_h = lax.broadcasted_iota(jnp.int32, (PITCH, LANES), 1)

    def layer1(d, carry):
        lhs = jnp.concatenate(
            [x1[d + a, b * PITCH : b * PITCH + rows1, :] for a in range(3) for b in range(3)], axis=1
        )
        y = jnp.dot(lhs, w1[...], preferred_element_type=jnp.float32)
        y = jnp.maximum(y + b1[...], 0.0)
        disp = d0 - 1 + d
        ok = jnp.where((disp >= 0) & (disp < NDISP), 1, 0)
        y = jnp.where(valid * ok > 0, y, 0.0)
        for hh in range(H + 2):
            z = y[hh * PITCH : (hh + 1) * PITCH]
            zr = pltpu.roll(z, C, 1)
            extra = jnp.where(lane_h < CH, pltpu.roll(zr, 1, 0), pltpu.roll(zr, PITCH - 1, 0))
            both = jnp.concatenate([z[:WROWS], extra[:WROWS]], axis=1)
            h2[d, hh * WROWS : (hh + 1) * WROWS, :] = both.astype(jnp.bfloat16)
        return carry

    lax.fori_loop(0, nd + 2, layer1, 0)

    rows2 = H * WROWS

    def layer2(d, carry):
        lhs = jnp.concatenate(
            [h2[d + a, b * WROWS : b * WROWS + rows2, :] for a in range(3) for b in range(3)], axis=1
        )
        ybuf[...] = jnp.dot(lhs, w2[...], preferred_element_type=jnp.float32) + b2[...]
        for i in range(WROWS):
            out_ref[d, :, i * LANES : (i + 1) * LANES] = ybuf[pl.ds(i, H, stride=WROWS), :]
        return carry

    lax.fori_loop(0, nd, layer2, 0)


def spread(kernel, depth):
    k = kernel.shape[3]
    cols = jnp.stack(
        [jnp.pad(kernel, ((0, 0), (0, 0), (j, COLS - 1 - j), (0, 0), (0, 0))) for j in range(COLS)], axis=4
    )
    cols = jnp.concatenate([cols[:, :, 1 : COLS + 1], cols[:, :, :1], cols[:, :, COLS + 1 :]], axis=2)
    mat = cols.reshape(9, (COLS + 2) * k, COLS * CH)
    mat = jnp.pad(mat, ((0, 0), (0, depth - mat.shape[1]), (0, 0)))
    return mat.reshape(9 * depth, COLS * CH)


def group_matrix():
    lane = jnp.arange(LANES)
    source = lane[:, None] // (C // G)
    target = jnp.where(
        lane < COLS * G,
        lane,
        jnp.where(
            lane < (COLS + 1) * G,
            lane - G,
            jnp.where(lane < (COLS + 2) * G, lane - (COLS + 1) * G, -1),
        ),
    )
    mat = jnp.where(source == target[None, :], 1.0 / (NPV * (C // G)), 0.0).astype(jnp.bfloat16)
    return jnp.concatenate([mat, mat], axis=0)


def on_device(
    ref_features, partner_lines, line_owner, line_index, line_offset, neighbours,
    conv1_weight, conv1_bias, conv2_weight, conv2_bias,
):
    n_tiles = lax.axis_size("tiles")
    views = lax.axis_size("views")
    nd = NDISP // views
    req = jnp.concatenate([line_owner[0, :, 0], line_index[0], line_offset[0]])
    req = jnp.pad(req, (0, LANES - req.shape[0])).astype(jnp.float32)
    req = jnp.broadcast_to(req[None], (8, LANES))
    body = NPV * H * LROWS + H * WROWS
    total = -(-(body + 16) // (16 * views)) * 16 * views
    vmem = pl.BlockSpec(memory_space=pltpu.VMEM)
    smem = pl.BlockSpec(memory_space=pltpu.SMEM)
    part = pl.pallas_call(
        partial(pack_kernel, views),
        out_shape=jax.ShapeDtypeStruct((total // views, LANES), jnp.bfloat16),
        in_specs=[vmem] * 3,
        out_specs=vmem,
        scratch_shapes=[pltpu.VMEM((total, LANES), jnp.float32)],
        compiler_params=pltpu.CompilerParams(vmem_limit_bytes=16 << 20),
        name="pack",
    )(partner_lines[0].reshape(NPV * H, SW * C), ref_features[0], req)
    gathered = lax.all_gather(part, ("tiles", "views"), axis=0, tiled=True).reshape(n_tiles, total, LANES)
    table = gathered[:, body, :].astype(jnp.int32).reshape(-1)
    nk = (nd + 4) // COLS
    f32, bf16 = jnp.float32, jnp.bfloat16
    out = pl.pallas_call(
        partial(main_kernel, n_tiles, nd),
        out_shape=jax.ShapeDtypeStruct((nd, H, W * CH), f32),
        in_specs=[smem, smem, pl.BlockSpec(memory_space=pl.ANY)] + [vmem] * 5,
        out_specs=vmem,
        scratch_shapes=[
            pltpu.VMEM((3 * NPV, HX, LROWS, LANES), bf16),
            pltpu.VMEM((3, HX * WROWS, LANES), bf16),
            pltpu.VMEM((3 * NPV, LPAD, LANES), f32),
            pltpu.VMEM((HX, 48, LANES), f32),
            pltpu.VMEM((2, HX, 16, LANES), f32),
            pltpu.VMEM((COLS, HX, 40, LANES), f32),
            pltpu.VMEM((COLS, 2, HX, 8, LANES), f32),
            pltpu.VMEM((HX, PITCH, LANES), f32),
            pltpu.VMEM((nk * COLS, HX * PITCH, LANES), bf16),
            pltpu.VMEM((nd + 2, (H + 2) * WROWS, 2 * LANES), bf16),
            pltpu.VMEM((H * WROWS, LANES), f32),
            pltpu.SemaphoreType.DMA,
            pltpu.SemaphoreType.DMA((9,)),
        ],
        compiler_params=pltpu.CompilerParams(vmem_limit_bytes=48 << 20),
        name="volume",
    )(
        table,
        neighbours.reshape(-1),
        gathered,
        spread(conv1_weight, LANES),
        jnp.tile(conv1_bias, COLS)[None],
        spread(conv2_weight, 2 * LANES),
        jnp.tile(conv2_bias, COLS)[None],
        group_matrix(),
    )
    return out[None]


def solution(mesh):
    return jax.shard_map(
        on_device,
        mesh=mesh,
        in_specs=(
            P("tiles", None, None),
            P("tiles", None, None, None),
            P("tiles", None, None),
            P("tiles", None),
            P("tiles", None),
            P(),
            P(),
            P(),
            P(),
            P(),
        ),
        out_specs=P("tiles", "views", None, None),
        check_vma=False,
    )
```

profile of v0, /device:TPU:1, one launch (start us, length us, event | category | flops | bytes accessed | tf_op | source)
XLA Modules:
  0.0 126.5 jit_solution(5546900132344290010)
XLA Ops:
  6.5 0.0 all-gather.2.cloned.1.call-start
  6.5 0.8 pad_add_fusion
  7.3 0.0 copy-start.1
  7.3 1.0 copy-done.1
  8.4 0.0 copy-start.2
  8.4 0.8 copy-done.2
  9.2 1.7 %pack.1 = bf16[592,128]{1,0:T(8,128)(2,1)} custom-call(bf16[32,8192]{1,0:T(8,128)(2,1)S(1)} %bitcast.30, bf16[8,4096]{1,0:T(8,128)(2,1)S(1)} %bitcast.31, f32[8,128]{1,0:T(8,128)S(1)} %broadcast_in_dim.21.req_ref), custom_call_target="tpu_custom_call" | custom-call | tf_op jit(solution)/shard_map/pack/pallas_call | solution.py:289
  10.9 0.0 all-gather.2.cloned.1.call-update
  11.0 1.9 %pad_bitcast_fusion = (bf16[3,3,6,32,1,32]{5,3,2,1,0,4:T(8,128)(2,1)S(1)}, bf16[3,3,6,32,1,32]{5,3,2,1,0,4:T(8,128)(2,1)S(1)}, bf16[3,3,6,32,1,32]{5,3,2,1,0,4:T(8,128)(2,1)S(1)}, bf16[3,3,6,32,1,32]{5,3,2,1,0,4:T(8,128)(2,1)S(1)}) fusion(bf16[3,3,3,32,32]{4,3,2,1,0:T(8,128)(2,1)} %param.18), kind=kLoop, calls=%fused_computation.42 | loop fusion | bytes 497664 | tf_op jit(solution)/shard_map/stack | solution.py:250
  12.9 0.5 pad_maximum_fusion
  13.3 0.2 slice.30
  13.6 0.5 fusion.8
  14.1 1.9 %copy.14 = bf16[3,3,6,32,4,32]{5,4,3,2,1,0:T(4,128)(2,1)S(1)} copy(bf16[3,3,6,32,4,32]{5,3,2,1,0,4:T(8,128)(2,1)S(1)} %fusion.8) | data formatting | bytes 884736 | tf_op jit(solution)/shard_map/concatenate | solution.py:253
  16.0 0.0 copy-start.3
  16.0 0.9 reshape.82
  16.9 0.0 copy-done.3
  16.9 0.1 pad_bitcast_fusion.4
  17.0 0.1 pad_maximum_fusion.3
  17.2 0.0 copy-start.4
  17.2 0.0 copy-start.5
  17.2 0.0 copy-start.6
  17.2 0.1 fusion.21
  17.3 0.2 copy.13
  17.5 0.2 reshape.80
  17.7 0.1 pad.54
  17.8 0.0 copy-done.4
  17.9 0.1 copy.12
  17.9 0.1 reshape.79.nb
  18.0 0.0 copy-done.5
  18.0 0.1 broadcast_in_dim_tile.6.b1
  18.1 0.0 copy-done.6
  18.1 0.1 broadcast_in_dim_tile.7.b2
  18.2 0.1 select_convert_fusion
  18.3 59.4 %all-gather.2.cloned.1.call-done = bf16[18944,128]{1,0:T(8,128)(2,1)} async-done(((bf16[592,128]{1,0:T(8,128)(2,1)}), bf16[18944,128]{1,0:T(8,128)(2,1)}) %all-gather.2.cloned.1.call-update) | async-done | bytes 4849680 | tf_op jit(solution)/shard_map/all_gather | solution.py:298
  77.7 0.7 slice_convert_fusion
  78.4 0.0 copy-start
  78.4 2.4 %copy-done = bf16[18944,128]{1,0:T(8,128)(2,1)S(1)} copy-done((bf16[18944,128]{1,0:T(8,128)(2,1)S(1)}, bf16[18944,128]{1,0:T(8,128)(2,1)}, u32[]{:S(2)}) %copy-start) | copy-done | bytes 4849688
  80.8 38.9 %volume.1 = f32[16,8,4096]{2,1,0:T(8,128)} custom-call(s32[1024]{0:T(1024)S(1)} %bitcast.32, s32[32]{0:T(128)S(1)} %reshape.79.nb, bf16[8,2368,128]{2,1,0:T(8,128)(2,1)S(1)} %bitcast.27, bf16[1152,128]{1,0:T(8,128)(2,1)S(1)} %bitcast.29, f32[1,128]{1,0:T(1,128)S(1)} %broadcast_in_dim_tile.6.b1, bf16[2304,128]{1,0:T(8,128)(2,1)S(1)} %bitcast.28, ...), custom_call_target="tpu_custom_call" | custom-call | tf_op jit(solution)/shard_map/volume/pallas_call | solution.py:302
  (8 shorter events, 0.1 us)
Async XLA Ops:
  6.5 71.2 %all-gather.2.cloned.1.call-start = ((), (), s32[]{:S(2)}) async-start(), calls=%async_computation | async-start | bytes 5001216 | tf_op jit(solution)/shard_map/all_gather | solution.py:298
  7.3 1.0 copy-start.1
  8.4 0.8 copy-start.2
  16.0 0.9 copy-start.3
  17.2 0.7 copy-start.4
  17.2 0.8 copy-start.5
  17.2 0.9 copy-start.6
  78.4 2.4 %copy-start = (bf16[18944,128]{1,0:T(8,128)(2,1)S(1)}, bf16[18944,128]{1,0:T(8,128)(2,1)}, u32[]{:S(2)}) copy-start(bf16[18944,128]{1,0:T(8,128)(2,1)} %all-gather.2.cloned.1.call-done) | copy-start | bytes 14548996
Sparse Core Ops, SparseCore 0:
  11.1 66.5 all-gather.1
where the time goes:
time: 127 us
  waiting for transfers between devices  59.4 us (47%)
  Pallas kernels  40.6 us (32%)
  between operations  13.6 us (11%)
  local copies, waits for them, and re-layouts  10.2 us (8%)
  other arithmetic  2.76 us (2%)
    all_gather x1, waiting for transfers between devices, on_device(): lax.all_gather(part, ('tiles', 'views'), axis=0, tiled=True)  59.4 us
    pallas_call x1, Pallas kernels, on_device(): pl.pallas_call(partial(main_kernel, n_tiles, nd), out_shape=jax.ShapeDtyp...  38.9 us
    unnamed x15, local copies, waits for them, and re-layouts  4.36 us
  transfers between devices with their start and end apart: 1, of which 1 were waited for; matrix products, arithmetic and copies ran while one was open for 6% of the time, Pallas kernels for 0%

commit v1 on v0

--- a/solution.py
+++ b/solution.py
@@ -2,6 +2,7 @@
 
 import jax
 import jax.numpy as jnp
+import numpy as np
 from jax import lax
 from jax.experimental import pallas as pl
 from jax.experimental.pallas import tpu as pltpu
@@ -23,9 +24,29 @@
 HX = H + 4
 FRONT = 8
 LPAD = FRONT + LROWS + 8
-
-
-def pack_kernel(views, lines_ref, ref_ref, req_ref, out_ref, scr):
+MESH = pl.DeviceIdType.MESH
+
+
+def spread_taps(raw_ref, out_ref, depth):
+    k = raw_ref.shape[0] // 27
+    group = lax.broadcasted_iota(jnp.int32, (k, LANES), 1) // CH
+    for ab in range(9):
+        taps = []
+        for e in range(3):
+            at = (ab * 3 + e) * k
+            tap = raw_ref[at : at + k, :].astype(jnp.float32)
+            taps.append(jnp.concatenate([tap] * COLS, axis=1))
+        rows = []
+        for c in list(range(COLS)) + [-1, COLS]:
+            row = jnp.zeros((k, LANES), jnp.float32)
+            for e in range(3):
+                row = jnp.where(group == c + 1 - e, taps[e], row)
+            rows.append(row)
+        rows.append(jnp.zeros((depth - len(rows) * k, LANES), jnp.float32))
+        out_ref[ab * depth : (ab + 1) * depth, :] = jnp.concatenate(rows, axis=0).astype(jnp.bfloat16)
+
+
+def pack_kernel(lines_ref, ref_ref, k1_ref, k2_ref, out_ref, w1_ref, w2_ref, scr):
     n_lines = lines_ref.shape[0]
     for j in range(LROWS):
         scr[pl.ds(j, n_lines, stride=LROWS), :] = lines_ref[:, j * LANES : (j + 1) * LANES].astype(jnp.float32)
@@ -33,17 +54,141 @@
     for i in range(WROWS):
         scr[pl.ds(base + i, H, stride=WROWS), :] = ref_ref[:, i * LANES : (i + 1) * LANES].astype(jnp.float32)
     base = base + H * WROWS
-    rest = scr.shape[0] - base
-    scr[base:, :] = jnp.concatenate([req_ref[...], jnp.zeros((rest - req_ref.shape[0], LANES), jnp.float32)], axis=0)
+    if scr.shape[0] > base:
+        scr[base:, :] = jnp.zeros((scr.shape[0] - base, LANES), jnp.float32)
     part = out_ref.shape[0]
     v = lax.axis_index("views")
     out_ref[...] = scr[pl.ds(pl.multiple_of(v * part, 16), part), :].astype(jnp.bfloat16)
+    spread_taps(k1_ref, w1_ref, LANES)
+    spread_taps(k2_ref, w2_ref, 2 * LANES)
+
+
+def gather_kernel(T, V, part_ref, req_ref, all_ref, tab_ref, own_sem, s1, r1, st, rt, s2, r2):
+    t = lax.axis_index("tiles")
+    v = lax.axis_index("views")
+    part = part_ref.shape[0]
+    hops = []
+    bit = V // 2
+    while bit >= 1:
+        hops.append(bit)
+        bit //= 2
+
+    def flip(view, bit):
+        return view + bit - 2 * bit * lax.rem(view // bit, 2)
+
+    def partner(bit):
+        return flip(v, bit)
+
+    barrier = pltpu.get_barrier_semaphore()
+
+    def greet(k, carry):
+        peer = lax.rem(t + k, T)
+        pl.semaphore_signal(barrier, inc=1, device_id=(peer, v), device_id_type=MESH)
+        return carry
+
+    lax.fori_loop(1, T, greet, 0)
+    for bit in hops:
+        pl.semaphore_signal(barrier, inc=1, device_id=(t, partner(bit)), device_id_type=MESH)
+    pl.semaphore_wait(barrier, T - 1 + len(hops))
+
+    def block(tile, view):
+        return all_ref.at[tile, pl.ds(pl.multiple_of(view * part, 16), part), :]
+
+    def table(peer, owner):
+        return pltpu.make_async_remote_copy(
+            src_ref=req_ref, dst_ref=tab_ref.at[owner], send_sem=st.at[peer], recv_sem=rt.at[owner],
+            device_id=(peer, v), device_id_type=MESH,
+        )
+
+    def direct(peer, owner):
+        return pltpu.make_async_remote_copy(
+            src_ref=part_ref, dst_ref=block(owner, v), send_sem=s1.at[peer], recv_sem=r1.at[owner],
+            device_id=(peer, v), device_id_type=MESH,
+        )
+
+    def start_direct(k, carry):
+        peer = lax.rem(t + k, T)
+        direct(peer, t).start()
+        table(peer, t).start()
+        return carry
+
+    def forward(h, tile, view, slot):
+        return pltpu.make_async_remote_copy(
+            src_ref=block(tile, view), dst_ref=block(tile, view),
+            send_sem=s2.at[h, slot, tile], recv_sem=r2.at[h, slot, tile],
+            device_id=(t, partner(hops[h])), device_id_type=MESH,
+        )
+
+    def views_before(h):
+        held = [(v, None)]
+        for g in range(h):
+            held = held + [(flip(view, hops[g]), (g, slot)) for slot, (view, _) in enumerate(held)]
+        return held
+
+    own_block = pltpu.make_async_copy(part_ref, block(t, v), own_sem.at[0])
+    own_table = pltpu.make_async_copy(req_ref, tab_ref.at[t], own_sem.at[1])
+    own_block.start()
+    own_table.start()
+    lax.fori_loop(1, T, start_direct, 0)
+    own_block.wait()
+    own_table.wait()
+
+    n_hops = len(hops)
+    final = views_before(n_hops)
+
+    def send_on(tile, slot):
+        view, came = final[slot]
+        first = 0 if came is None else came[0] + 1
+        for h in range(first, n_hops):
+            forward(h, tile, view, slot).start()
+
+    def land(tile, slot):
+        view, came = final[slot]
+        h, sent_slot = came
+        forward(h, tile, view, sent_slot).wait_recv()
+        send_on(tile, slot)
+
+    def step(k, carry):
+        tile = lax.rem(t - k + T, T)
+        direct(tile, tile).wait_recv()
+        send_on(tile, 0)
+        before = lax.rem(tile + 1, T)
+        for slot in range(1, len(final)):
+            land(before, slot)
+        return carry
+
+    send_on(t, 0)
+    lax.fori_loop(1, T, step, 0)
+    last = lax.rem(t + 1, T)
+    for slot in range(1, len(final)):
+        land(last, slot)
+
+    def finish(k, carry):
+        tile = lax.rem(t + k, T)
+        direct(tile, t).wait_send()
+        table(tile, t).wait_send()
+        table(tile, tile).wait_recv()
+        return carry
+
+    lax.fori_loop(1, T, finish, 0)
+
+    def finish_forward(tile, carry):
+        for slot in range(len(final)):
+            view, came = final[slot]
+            first = 0 if came is None else came[0] + 1
+            for h in range(first, n_hops):
+                forward(h, tile, view, slot).wait_send()
+        return carry
+
+    lax.fori_loop(0, T, finish_forward, 0)
 
 
 def main_kernel(
-    n_tiles, nd, req, nb, all_ref, w1, b1, w2, b2, gm, out_ref,
-    lines, refb, linef, vt0, vte0, vt, vte, refx, x1, h2, ybuf, sem_l, sem_r,
+    nd, nb, tab_ref, all_ref, w1, b1, w2, b2, gm, out_ref,
+    tab, lines, refb, linef, vt0, vte0, vt, vte, refx, x1, h2, ybuf, sem_l, sem_r, sem_t,
 ):
+    table_copy = pltpu.make_async_copy(tab_ref, tab, sem_t)
+    table_copy.start()
     t = lax.axis_index("tiles")
     v = lax.axis_index("views")
     d0 = v * nd
@@ -78,14 +223,15 @@
     def row_of(hh):
         return jnp.where(hh < 2, hh + H - 2, jnp.where(hh < H + 2, hh - 2, hh - H - 2))
 
+    table_copy.wait()
+
     def fetch(hh, carry):
         row = row_of(hh)
         for s in range(3):
             tt = tile_of(s, hh)
             for u in range(NPV):
-                j = tt * LANES + u * H + row
-                owner = req[j]
-                index = req[j + NPV * H]
+                owner = tab[tt, 0, u * H + row]
+                index = tab[tt, 0, NPV * H + u * H + row]
                 src = pl.multiple_of((u * H + index) * LROWS, LROWS)
                 pltpu.make_async_copy(
                     all_ref.at[owner, pl.ds(src, LROWS), :], lines.at[s * NPV + u, hh], sem_l
@@ -126,7 +272,7 @@
             tt = tile_of(s, hh)
             total = None
             for u in range(NPV):
-                off = req[tt * LANES + 2 * NPV * H + u * H + row]
+                off = tab[tt, 0, 2 * NPV * H + u * H + row]
                 col = off + d0 - 2 + FRONT * COLS
                 q = lax.div(col, COLS)
                 r0 = col - q * COLS
@@ -150,7 +296,11 @@
 
     lane1 = lax.broadcasted_iota(jnp.int32, (1, LANES), 1)
 
-    def shift_all(hh, carry):
+    lane_p = lax.broadcasted_iota(jnp.int32, (PITCH, LANES), 1)
+    edge3 = lax.broadcasted_iota(jnp.int32, (16, LANES), 0) == 0
+    nk = (nd + 4) // COLS
+
+    def cost_row(hh, carry):
         for r in range(COLS):
             keep = lane1 < LANES - C * r
 
@@ -160,29 +310,21 @@
                 s = LANES - C * r
                 return jnp.where(keep, pltpu.roll(x, s, 1), pltpu.roll(y, s, 1))
 
-            vt[r, hh] = moved(vt0[hh, 0:40, :], vt0[hh, 1:41, :])
+            vt[r] = moved(vt0[hh, 0:40, :], vt0[hh, 1:41, :])
             for side in range(2):
-                vte[r, side, hh] = moved(vte0[side, hh, 0:8, :], vte0[side, hh, 1:9, :])
-        return carry
-
-    lax.fori_loop(0, HX, shift_all, 0)
-
-    lane_p = lax.broadcasted_iota(jnp.int32, (PITCH, LANES), 1)
-    edge3 = lax.broadcasted_iota(jnp.int32, (16, LANES), 0) == 0
-    nk = (nd + 4) // COLS
-    for k in range(nk):
-        def cost_row(hh, carry, k=k):
+                vte[r, side] = moved(vte0[side, hh, 0:8, :], vte0[side, hh, 1:9, :])
+        ref_rows = refx[hh]
+        at = pl.multiple_of(hh * PITCH, 16)
+        for k in range(nk):
             parts = []
-            ref_rows = refx[hh]
             for r in range(COLS):
-                own = vt[r, hh, k : k + WROWS, :]
-                side = jnp.where(edge3, vte[r, 1, hh, k : k + 1, :], vte[r, 0, hh, k : k + 1, :])
+                own = vt[r, k : k + WROWS, :]
+                side = jnp.where(edge3, vte[r, 1, k : k + 1, :], vte[r, 0, k : k + 1, :])
                 prod = ref_rows * jnp.concatenate([own, side], axis=0)
                 top = prod.astype(jnp.bfloat16)
                 low = (prod - top.astype(jnp.float32)).astype(jnp.bfloat16)
                 parts.append(jnp.concatenate([top, low], axis=1))
             cost = jnp.dot(jnp.concatenate(parts, axis=0), gm[...], preferred_element_type=jnp.float32)
-            at = pl.multiple_of(hh * PITCH, 16)
             for r in range(COLS):
                 c = cost[r * PITCH : (r + 1) * PITCH]
                 x = jnp.where(
@@ -194,9 +336,9 @@
                 disp = d0 - 2 + dd
                 x = jnp.where((disp >= 0) & (disp < NDISP), x, 0.0)
                 x1[dd, pl.ds(at, PITCH), :] = x.astype(jnp.bfloat16)
-            return carry
-
-        lax.fori_loop(0, HX, cost_row, 0)
+        return carry
+
+    lax.fori_loop(0, HX, cost_row, 0)
 
     rows1 = (H + 2) * PITCH
     row_id = lax.broadcasted_iota(jnp.int32, (rows1, LANES), 0)
@@ -229,47 +371,42 @@
             h2[d, hh * WROWS : (hh + 1) * WROWS, :] = both.astype(jnp.bfloat16)
         return carry
 
-    lax.fori_loop(0, nd + 2, layer1, 0)
+    def layer1_pair(i, carry):
+        layer1(2 * i, carry)
+        layer1(2 * i + 1, carry)
+        return carry
+
+    lax.fori_loop(0, (nd + 2) // 2, layer1_pair, 0)
 
     rows2 = H * WROWS
 
-    def layer2(d, carry):
+    def layer2(d, slot):
         lhs = jnp.concatenate(
             [h2[d + a, b * WROWS : b * WROWS + rows2, :] for a in range(3) for b in range(3)], axis=1
         )
-        ybuf[...] = jnp.dot(lhs, w2[...], preferred_element_type=jnp.float32) + b2[...]
+        y = ybuf.at[slot]
+        y[...] = jnp.dot(lhs, w2[...], preferred_element_type=jnp.float32) + b2[...]
         for i in range(WROWS):
-            out_ref[d, :, i * LANES : (i + 1) * LANES] = ybuf[pl.ds(i, H, stride=WROWS), :]
-        return carry
-
-    lax.fori_loop(0, nd, layer2, 0)
-
-
-def spread(kernel, depth):
-    k = kernel.shape[3]
-    cols = jnp.stack(
-        [jnp.pad(kernel, ((0, 0), (0, 0), (j, COLS - 1 - j), (0, 0), (0, 0))) for j in range(COLS)], axis=4
-    )
-    cols = jnp.concatenate([cols[:, :, 1 : COLS + 1], cols[:, :, :1], cols[:, :, COLS + 1 :]], axis=2)
-    mat = cols.reshape(9, (COLS + 2) * k, COLS * CH)
-    mat = jnp.pad(mat, ((0, 0), (0, depth - mat.shape[1]), (0, 0)))
-    return mat.reshape(9 * depth, COLS * CH)
+            out_ref[d, :, i * LANES : (i + 1) * LANES] = y[pl.ds(i, H, stride=WROWS), :]
+
+    def layer2_pair(i, carry):
+        layer2(2 * i, 0)
+        layer2(2 * i + 1, 1)
+        return carry
+
+    lax.fori_loop(0, nd // 2, layer2_pair, 0)
 
 
 def group_matrix():
-    lane = jnp.arange(LANES)
+    lane = np.arange(LANES)
     source = lane[:, None] // (C // G)
-    target = jnp.where(
-        lane < COLS * G,
-        lane,
-        jnp.where(
-            lane < (COLS + 1) * G,
-            lane - G,
-            jnp.where(lane < (COLS + 2) * G, lane - (COLS + 1) * G, -1),
-        ),
-    )
-    mat = jnp.where(source == target[None, :], 1.0 / (NPV * (C // G)), 0.0).astype(jnp.bfloat16)
-    return jnp.concatenate([mat, mat], axis=0)
+    target = np.full((LANES,), -1)
+    own = COLS * G
+    target[:own] = lane[:own]
+    target[own : own + G] = lane[own - G : own]
+    target[own + G : own + 2 * G] = lane[:G]
+    mat = np.where(source == target[None, :], 1.0 / (NPV * (C // G)), 0.0)
+    return jnp.asarray(np.concatenate([mat, mat], axis=0), jnp.bfloat16)
 
 
 def on_device(
@@ -280,54 +417,80 @@
     views = lax.axis_size("views")
     nd = NDISP // views
     req = jnp.concatenate([line_owner[0, :, 0], line_index[0], line_offset[0]])
-    req = jnp.pad(req, (0, LANES - req.shape[0])).astype(jnp.float32)
-    req = jnp.broadcast_to(req[None], (8, LANES))
+    req = jnp.broadcast_to(jnp.pad(req, (0, LANES - req.shape[0]))[None], (8, LANES))
     body = NPV * H * LROWS + H * WROWS
-    total = -(-(body + 16) // (16 * views)) * 16 * views
+    total = -(-body // (16 * views)) * 16 * views
     vmem = pl.BlockSpec(memory_space=pltpu.VMEM)
     smem = pl.BlockSpec(memory_space=pltpu.SMEM)
-    part = pl.pallas_call(
-        partial(pack_kernel, views),
-        out_shape=jax.ShapeDtypeStruct((total // views, LANES), jnp.bfloat16),
-        in_specs=[vmem] * 3,
-        out_specs=vmem,
+    hbm = pl.BlockSpec(memory_space=pl.ANY)
+    part, w1, w2 = pl.pallas_call(
+        pack_kernel,
+        out_shape=[
+            jax.ShapeDtypeStruct((total // views, LANES), jnp.bfloat16),
+            jax.ShapeDtypeStruct((9 * LANES, LANES), jnp.bfloat16),
+            jax.ShapeDtypeStruct((18 * LANES, LANES), jnp.bfloat16),
+        ],
+        in_specs=[vmem] * 4,
+        out_specs=[vmem] * 3,
         scratch_shapes=[pltpu.VMEM((total, LANES), jnp.float32)],
         compiler_params=pltpu.CompilerParams(vmem_limit_bytes=16 << 20),
         name="pack",
-    )(partner_lines[0].reshape(NPV * H, SW * C), ref_features[0], req)
-    gathered = lax.all_gather(part, ("tiles", "views"), axis=0, tiled=True).reshape(n_tiles, total, LANES)
-    table = gathered[:, body, :].astype(jnp.int32).reshape(-1)
+    )(
+        partner_lines[0].reshape(NPV * H, SW * C),
+        ref_features[0],
+        conv1_weight.reshape(27 * G, CH),
+        conv2_weight.reshape(27 * CH, CH),
+    )
+    hops = max(1, views.bit_length() - 1)
+    dma = pltpu.SemaphoreType.DMA
+    gathered, table = pl.pallas_call(
+        partial(gather_kernel, n_tiles, views),
+        out_shape=[
+            jax.ShapeDtypeStruct((n_tiles, total, LANES), jnp.bfloat16),
+            jax.ShapeDtypeStruct((n_tiles, 8, LANES), jnp.int32),
+        ],
+        in_specs=[hbm, hbm],
+        out_specs=[hbm, hbm],
+        scratch_shapes=[
+            dma((2,)), dma((n_tiles,)), dma((n_tiles,)), dma((n_tiles,)), dma((n_tiles,)),
+            dma((hops, views, n_tiles)), dma((hops, views, n_tiles)),
+        ],
+        compiler_params=pltpu.CompilerParams(collective_id=0, has_side_effects=True),
+        name="gather",
+    )(part, req)
     nk = (nd + 4) // COLS
     f32, bf16 = jnp.float32, jnp.bfloat16
     out = pl.pallas_call(
-        partial(main_kernel, n_tiles, nd),
+        partial(main_kernel, nd),
         out_shape=jax.ShapeDtypeStruct((nd, H, W * CH), f32),
-        in_specs=[smem, smem, pl.BlockSpec(memory_space=pl.ANY)] + [vmem] * 5,
+        in_specs=[smem, hbm, hbm] + [vmem] * 5,
         out_specs=vmem,
         scratch_shapes=[
+            pltpu.SMEM((n_tiles, 8, LANES), jnp.int32),
             pltpu.VMEM((3 * NPV, HX, LROWS, LANES), bf16),
             pltpu.VMEM((3, HX * WROWS, LANES), bf16),
             pltpu.VMEM((3 * NPV, LPAD, LANES), f32),
             pltpu.VMEM((HX, 48, LANES), f32),
             pltpu.VMEM((2, HX, 16, LANES), f32),
-            pltpu.VMEM((COLS, HX, 40, LANES), f32),
-            pltpu.VMEM((COLS, 2, HX, 8, LANES), f32),
+            pltpu.VMEM((COLS, 40, LANES), f32),
+            pltpu.VMEM((COLS, 2, 8, LANES), f32),
             pltpu.VMEM((HX, PITCH, LANES), f32),
             pltpu.VMEM((nk * COLS, HX * PITCH, LANES), bf16),
             pltpu.VMEM((nd + 2, (H + 2) * WROWS, 2 * LANES), bf16),
-            pltpu.VMEM((H * WROWS, LANES), f32),
-            pltpu.SemaphoreType.DMA,
-            pltpu.SemaphoreType.DMA((9,)),
+            pltpu.VMEM((2, H * WROWS, LANES), f32),
+            dma,
+            dma((9,)),
+            dma,
         ],
         compiler_params=pltpu.CompilerParams(vmem_limit_bytes=48 << 20),
         name="volume",
     )(
+        neighbours.reshape(-1),
         table,
-        neighbours.reshape(-1),
         gathered,
-        spread(conv1_weight, LANES),
+        w1,
         jnp.tile(conv1_bias, COLS)[None],
-        spread(conv2_weight, 2 * LANES),
+        w2,
         jnp.tile(conv2_bias, COLS)[None],
         group_matrix(),
     )

time: 127 us -> 92.7 us (0.73)
  the two profiles are of different devices: /device:TPU:1 before, /device:TPU:19 now
where the time goes in v1:
time: 92.7 us; the launch traced here: 92.3 us
  Pallas kernels  80.3 us (87%)
  local copies, waits for them, and re-layouts  11.1 us (12%)
    pallas_call x1, Pallas kernels, on_device(): pl.pallas_call(partial(gather_kernel, n_tiles, views), out_shape=[jax.Sha...  49.9 us
    pallas_call x1, Pallas kernels, on_device(): pl.pallas_call(partial(main_kernel, nd), out_shape=jax.ShapeDtypeStruct((...  29 us
    unnamed x17, local copies, waits for them, and re-layouts  8.97 us

profile of v1, /device:TPU:19, one launch (start us, length us, event | category | flops | bytes accessed | tf_op | source)
XLA Modules:
  0.0 92.3 jit_solution(13884287032363395111)
XLA Ops:
  0.0 0.8 pad_add_fusion
  0.8 0.7 tile.4
  1.4 0.1 broadcast_in_dim_tile.6.b1
  1.5 0.7 tile.5
  2.2 0.1 broadcast_in_dim_tile.7.b2
  2.3 0.6 broadcast_in_dim.4.req_ref
  2.8 0.8 copy.13
  3.6 0.1 reshape.12.nb
  3.7 0.0 copy-start.1
  3.7 1.0 %copy-done.1 = bf16[1,4,8,8192]{3,2,1,0:T(8,128)(2,1)S(1)} copy-done((bf16[1,4,8,8192]{3,2,1,0:T(8,128)(2,1)S(1)}, bf16[1,4,8,8192]{3,2,1,0:T(8,128)(2,1)}, u32[]{:S(2)}) %copy-start.1) | copy-done | bytes 524312
  4.7 0.0 copy-start.2
  4.7 0.9 %copy-done.2 = bf16[3,3,3,32,32]{4,3,2,1,0:T(8,128)(2,1)S(1)} copy-done((bf16[3,3,3,32,32]{4,3,2,1,0:T(8,128)(2,1)S(1)}, bf16[3,3,3,32,32]{4,3,2,1,0:T(8,128)(2,1)}, u32[]{:S(2)}) %copy-start.2) | copy-done | bytes 55320
  5.7 0.0 copy-start.5
  5.7 0.8 copy-done.5
  6.5 0.0 copy-start.6
  6.5 0.8 copy-done.6
  7.3 1.4 %pack.1 = (bf16[576,128]{1,0:T(8,128)(2,1)S(1)}, bf16[1152,128]{1,0:T(8,128)(2,1)S(1)}, bf16[2304,128]{1,0:T(8,128)(2,1)S(1)}) custom-call(bf16[32,8192]{1,0:T(8,128)(2,1)S(1)} %bitcast.8, bf16[8,4096]{1,0:T(8,128)(2,1)S(1)} %bitcast.10, bf16[216,32]{1,0:T(8,128)(2,1)S(1)} %bitcast.11, bf16[864,32]{1,0:T(8,128)(2,1)S(1)} %bitcast.9), custom_call_target="tpu_custom_call" | custom-call | tf_op jit(solution)/shard_map/pack/pallas_call | solution.py:426
  8.7 0.0 copy-start.3
  8.7 0.7 copy-done.3
  9.4 49.9 %gather.1 = (bf16[8,2304,128]{2,1,0:T(8,128)(2,1)}, s32[8,8,128]{2,1,0:T(8,128)}) custom-call(bf16[576,128]{1,0:T(8,128)(2,1)} %copy-done.3, s32[8,128]{1,0:T(8,128)} %broadcast_in_dim.4.req_ref), custom_call_target="tpu_custom_call" | custom-call | tf_op jit(solution)/shard_map/gather/pallas_call | solution.py:446
  59.3 0.0 copy-start
  59.3 2.3 %copy-done = bf16[8,2304,128]{2,1,0:T(8,128)(2,1)S(1)} copy-done((bf16[8,2304,128]{2,1,0:T(8,128)(2,1)S(1)}, bf16[8,2304,128]{2,1,0:T(8,128)(2,1)}, u32[]{:S(2)}) %copy-start) | copy-done | bytes 4718616
  61.7 0.0 copy-start.4
  61.7 0.8 copy-done.4
  62.5 0.0 copy-start.7
  62.5 0.8 copy-done.7
  63.3 29.0 %volume.1 = f32[16,8,4096]{2,1,0:T(8,128)} custom-call(s32[32]{0:T(128)S(1)} %reshape.12.nb, s32[8,8,128]{2,1,0:T(8,128)S(1)} %copy-done.7, bf16[8,2304,128]{2,1,0:T(8,128)(2,1)S(1)} %copy-done, bf16[1152,128]{1,0:T(8,128)(2,1)S(1)} %get-tuple-element.13.w1, f32[1,128]{1,0:T(1,128)S(1)} %broadcast_in_dim_tile.6.b1, ...), custom_call_target="tpu_custom_call" | custom-call | tf_op jit(solution)/shard_map/volume/pallas_call | solution.py:463
  (1 shorter events, 0.0 us)
Async XLA Ops:
  3.7 1.0 %copy-start.1 = (bf16[1,4,8,8192]{3,2,1,0:T(8,128)(2,1)S(1)}, bf16[1,4,8,8192]{3,2,1,0:T(8,128)(2,1)}, u32[]{:S(2)}) copy-start(bf16[1,4,8,8192]{3,2,1,0:T(8,128)(2,1)} %param.12) | copy-start | bytes 1572868
  4.7 0.9 %copy-start.2 = (bf16[3,3,3,32,32]{4,3,2,1,0:T(8,128)(2,1)S(1)}, bf16[3,3,3,32,32]{4,3,2,1,0:T(8,128)(2,1)}, u32[]{:S(2)}) copy-start(bf16[3,3,3,32,32]{4,3,2,1,0:T(8,128)(2,1)} %param.19) | copy-start | bytes 165892
  5.7 0.8 copy-start.5
  6.5 0.8 copy-start.6
  8.7 0.7 copy-start.3
  59.3 2.3 %copy-start = (bf16[8,2304,128]{2,1,0:T(8,128)(2,1)S(1)}, bf16[8,2304,128]{2,1,0:T(8,128)(2,1)}, u32[]{:S(2)}) copy-start(bf16[8,2304,128]{2,1,0:T(8,128)(2,1)} %get-tuple-element.12.all_ref) | copy-start | bytes 14155780
  61.7 0.8 copy-start.4
  62.5 0.8 copy-start.7

commit v2 on v1

--- a/solution.py
+++ b/solution.py
@@ -1,8 +1,8 @@
+import heapq
 from functools import partial
 
 import jax
 import jax.numpy as jnp
-import numpy as np
 from jax import lax
 from jax.experimental import pallas as pl
 from jax.experimental.pallas import tpu as pltpu
@@ -27,7 +27,7 @@
 MESH = pl.DeviceIdType.MESH
 
 
-def spread_taps(raw_ref, out_ref, depth):
+def spread_taps(raw_ref, out_ref, depth, pitch):
     k = raw_ref.shape[0] // 27
     group = lax.broadcasted_iota(jnp.int32, (k, LANES), 1) // CH
     for ab in range(9):
@@ -43,10 +43,15 @@
                 row = jnp.where(group == c + 1 - e, taps[e], row)
             rows.append(row)
         rows.append(jnp.zeros((depth - len(rows) * k, LANES), jnp.float32))
-        out_ref[ab * depth : (ab + 1) * depth, :] = jnp.concatenate(rows, axis=0).astype(jnp.bfloat16)
-
-
-def pack_kernel(lines_ref, ref_ref, k1_ref, k2_ref, out_ref, w1_ref, w2_ref, scr):
+        at = ab // 3 * pitch + ab % 3 * depth
+        out_ref[at : at + depth, :] = jnp.concatenate(rows, axis=0).astype(jnp.bfloat16)
+    if pitch > 3 * depth:
+        for a in range(3):
+            out_ref[a * pitch + 3 * depth : (a + 1) * pitch, :] = jnp.zeros((pitch - 3 * depth, LANES), jnp.bfloat16)
+
+
+def pack_kernel(lines_ref, ref_ref, k1_ref, k2_ref, req_ref, out_ref, w1_ref, w2_ref, req8_ref, scr):
+    req8_ref[...] = jnp.broadcast_to(req_ref[...], req8_ref.shape)
     n_lines = lines_ref.shape[0]
     for j in range(LROWS):
         scr[pl.ds(j, n_lines, stride=LROWS), :] = lines_ref[:, j * LANES : (j + 1) * LANES].astype(jnp.float32)
@@ -59,133 +64,112 @@
     part = out_ref.shape[0]
     v = lax.axis_index("views")
     out_ref[...] = scr[pl.ds(pl.multiple_of(v * part, 16), part), :].astype(jnp.bfloat16)
-    spread_taps(k1_ref, w1_ref, LANES)
-    spread_taps(k2_ref, w2_ref, 2 * LANES)
-
-
-def gather_kernel(T, V, part_ref, req_ref, all_ref, tab_ref, own_sem, s1, r1, st, rt, s2, r2):
+    spread_taps(k1_ref, w1_ref, LANES // 2, 2 * LANES)
+    spread_taps(k2_ref, w2_ref, 2 * LANES, 6 * LANES)
+
+
+def hop_orders(T, V):
+    def bits(axis, size):
+        out = []
+        while size > 1:
+            size //= 2
+            out.append((axis, size))
+        return out
+
+    tb, vb = bits(0, T), bits(1, V)
+    first = tb + vb
+    second = tb[:-1] + vb[:1] + tb[-1:] + vb[1:]
+    return first, second, tb
+
+
+def arrivals(orders, costs):
+    free = {}
+    heap = [(0.0, o, 0) for o in range(len(orders))]
+    seen = []
+    while heap:
+        now, o, mask = heapq.heappop(heap)
+        seen.append((o, mask))
+        for h in range(mask.bit_length(), len(orders[o])):
+            hop = orders[o][h]
+            free[hop] = max(free.get(hop, 0.0), now) + costs[o] * (0.2 if hop == (1, 1) else 1.0)
+            heapq.heappush(heap, (free[hop], o, mask | (1 << h)))
+    return seen
+
+
+def gather_kernel(T, V, part_ref, req_ref, all_ref, tab_ref, own_sem, *sems):
     t = lax.axis_index("tiles")
     v = lax.axis_index("views")
     part = part_ref.shape[0]
-    hops = []
-    bit = V // 2
-    while bit >= 1:
-        hops.append(bit)
-        bit //= 2
-
-    def flip(view, bit):
-        return view + bit - 2 * bit * lax.rem(view // bit, 2)
-
-    def partner(bit):
-        return flip(v, bit)
+    half = part // 2
+    orders = hop_orders(T, V)
+
+    def flip(x, bit):
+        return x + bit - 2 * bit * lax.rem(lax.div(x, bit), 2)
+
+    def across(mask, order):
+        at = [t, v]
+        for h, (axis, bit) in enumerate(order):
+            if mask >> h & 1:
+                at[axis] = flip(at[axis], bit)
+        return tuple(at)
 
     barrier = pltpu.get_barrier_semaphore()
-
-    def greet(k, carry):
-        peer = lax.rem(t + k, T)
-        pl.semaphore_signal(barrier, inc=1, device_id=(peer, v), device_id_type=MESH)
-        return carry
-
-    lax.fori_loop(1, T, greet, 0)
-    for bit in hops:
-        pl.semaphore_signal(barrier, inc=1, device_id=(t, partner(bit)), device_id_type=MESH)
-    pl.semaphore_wait(barrier, T - 1 + len(hops))
-
-    def block(tile, view):
-        return all_ref.at[tile, pl.ds(pl.multiple_of(view * part, 16), part), :]
-
-    def table(peer, owner):
+    hops = orders[0]
+    for hop in hops:
+        pl.semaphore_signal(barrier, inc=1, device_id=across(1, [hop]), device_id_type=MESH)
+    pl.semaphore_wait(barrier, len(hops))
+
+    def place(o, mask):
+        tile, view = across(mask, orders[o])
+        if o == 2:
+            return tab_ref.at[tile]
+        return all_ref.at[tile, pl.ds(pl.multiple_of(view * part + o * half, 16), half), :]
+
+    def source(o):
+        return req_ref if o == 2 else part_ref.at[pl.ds(o * half, half), :]
+
+    def send(o, mask, h):
         return pltpu.make_async_remote_copy(
-            src_ref=req_ref, dst_ref=tab_ref.at[owner], send_sem=st.at[peer], recv_sem=rt.at[owner],
-            device_id=(peer, v), device_id_type=MESH,
+            src_ref=source(o) if mask == 0 else place(o, mask),
+            dst_ref=place(o, mask),
+            send_sem=sems[2 * o].at[mask | (1 << h)],
+            recv_sem=sems[2 * o + 1].at[mask | (1 << h)],
+            device_id=across(1 << h, orders[o]),
+            device_id_type=MESH,
         )
 
-    def direct(peer, owner):
+    def landed(o, mask):
         return pltpu.make_async_remote_copy(
-            src_ref=part_ref, dst_ref=block(owner, v), send_sem=s1.at[peer], recv_sem=r1.at[owner],
-            device_id=(peer, v), device_id_type=MESH,
+            src_ref=place(o, mask),
+            dst_ref=place(o, mask),
+            send_sem=sems[2 * o].at[mask],
+            recv_sem=sems[2 * o + 1].at[mask],
+            device_id=across(1, orders[o]),
+            device_id_type=MESH,
         )
 
-    def start_direct(k, carry):
-        peer = lax.rem(t + k, T)
-        direct(peer, t).start()
-        table(peer, t).start()
-        return carry
-
-    def forward(h, tile, view, slot):
-        return pltpu.make_async_remote_copy(
-            src_ref=block(tile, view), dst_ref=block(tile, view),
-            send_sem=s2.at[h, slot, tile], recv_sem=r2.at[h, slot, tile],
-            device_id=(t, partner(hops[h])), device_id_type=MESH,
-        )
-
-    def views_before(h):
-        held = [(v, None)]
-        for g in range(h):
-            held = held + [(flip(view, hops[g]), (g, slot)) for slot, (view, _) in enumerate(held)]
-        return held
-
-    own_block = pltpu.make_async_copy(part_ref, block(t, v), own_sem.at[0])
-    own_table = pltpu.make_async_copy(req_ref, tab_ref.at[t], own_sem.at[1])
-    own_block.start()
-    own_table.start()
-    lax.fori_loop(1, T, start_direct, 0)
-    own_block.wait()
-    own_table.wait()
-
-    n_hops = len(hops)
-    final = views_before(n_hops)
-
-    def send_on(tile, slot):
-        view, came = final[slot]
-        first = 0 if came is None else came[0] + 1
-        for h in range(first, n_hops):
-            forward(h, tile, view, slot).start()
-
-    def land(tile, slot):
-        view, came = final[slot]
-        h, sent_slot = came
-        forward(h, tile, view, sent_slot).wait_recv()
-        send_on(tile, slot)
-
-    def step(k, carry):
-        tile = lax.rem(t - k + T, T)
-        direct(tile, tile).wait_recv()
-        send_on(tile, 0)
-        before = lax.rem(tile + 1, T)
-        for slot in range(1, len(final)):
-            land(before, slot)
-        return carry
-
-    send_on(t, 0)
-    lax.fori_loop(1, T, step, 0)
-    last = lax.rem(t + 1, T)
-    for slot in range(1, len(final)):
-        land(last, slot)
-
-    def finish(k, carry):
-        tile = lax.rem(t + k, T)
-        direct(tile, t).wait_send()
-        table(tile, t).wait_send()
-        table(tile, tile).wait_recv()
-        return carry
-
-    lax.fori_loop(1, T, finish, 0)
-
-    def finish_forward(tile, carry):
-        for slot in range(len(final)):
-            view, came = final[slot]
-            first = 0 if came is None else came[0] + 1
-            for h in range(first, n_hops):
-                forward(h, tile, view, slot).wait_send()
-        return carry
-
-    lax.fori_loop(0, T, finish_forward, 0)
+    sent = []
+    own = []
+    for o, mask in arrivals(orders, (1.0, 1.0, 0.02)):
+        if mask:
+            landed(o, mask).wait_recv()
+        for h in range(mask.bit_length(), len(orders[o])):
+            copy = send(o, mask, h)
+            copy.start()
+            sent.append(copy)
+        if mask == 0:
+            mine = pltpu.make_async_copy(source(o), place(o, 0), own_sem.at[o])
+            mine.start()
+            own.append(mine)
+    for copy in own:
+        copy.wait()
+    for copy in sent:
+        copy.wait_send()
 
 
 def main_kernel(
-    nd, nb, tab_ref, all_ref, w1, b1, w2, b2, gm, out_ref,
-    tab, lines, refb, linef, vt0, vte0, vt, vte, refx, x1, h2, ybuf, sem_l, sem_r, sem_t,
+    nd, nb, tab_ref, all_ref, w1, b1, w2, b2, out_ref,
+    tab, lines, refb, linef, vt0, vte0, vt, vte, refx, xprev, x1, h2, ybuf, sem_l, sem_r, sem_t,
 ):
     table_copy = pltpu.make_async_copy(tab_ref, tab, sem_t)
     table_copy.start()
@@ -194,7 +178,7 @@
     d0 = v * nd
 
     def link(x, side):
-        got = nb[jnp.maximum(x, 0) * 4 + side]
+        got = nb[jnp.maximum(x, 0), side]
         return jnp.where(x >= 0, got, -1)
 
     mids = [t, link(t, 2), link(t, 3)]
@@ -298,7 +282,9 @@
 
     lane_p = lax.broadcasted_iota(jnp.int32, (PITCH, LANES), 1)
     edge3 = lax.broadcasted_iota(jnp.int32, (16, LANES), 0) == 0
+    lane_half = lax.rem(lane_p, LANES // 2)
     nk = (nd + 4) // COLS
+    gm = group_matrix()
 
     def cost_row(hh, carry):
         for r in range(COLS):
@@ -324,21 +310,26 @@
                 top = prod.astype(jnp.bfloat16)
                 low = (prod - top.astype(jnp.float32)).astype(jnp.bfloat16)
                 parts.append(jnp.concatenate([top, low], axis=1))
-            cost = jnp.dot(jnp.concatenate(parts, axis=0), gm[...], preferred_element_type=jnp.float32)
+            cost = jnp.dot(jnp.concatenate(parts, axis=0), gm, preferred_element_type=jnp.float32)
             for r in range(COLS):
                 c = cost[r * PITCH : (r + 1) * PITCH]
                 x = jnp.where(
-                    lane_p < COLS * G,
+                    lane_half < COLS * G,
                     c,
-                    jnp.where(lane_p < (COLS + 1) * G, pltpu.roll(c, 1, 0), pltpu.roll(c, PITCH - 1, 0)),
+                    jnp.where(lane_half < (COLS + 1) * G, pltpu.roll(c, 1, 0), pltpu.roll(c, PITCH - 1, 0)),
                 )
                 dd = k * COLS + r
-                disp = d0 - 2 + dd
-                x = jnp.where((disp >= 0) & (disp < NDISP), x, 0.0)
-                x1[dd, pl.ds(at, PITCH), :] = x.astype(jnp.bfloat16)
+                if dd < 2 or dd >= nd + 2:
+                    disp = d0 - 2 + dd
+                    x = jnp.where((disp >= 0) & (disp < NDISP), x, 0.0)
+                both = jnp.where(lane_p < LANES // 2, xprev[dd], x)
+                x1[dd, pl.ds(at, PITCH), :] = both.astype(jnp.bfloat16)
+                xprev[dd] = x
         return carry
 
     lax.fori_loop(0, HX, cost_row, 0)
+    for dd in range(nk * COLS):
+        x1[dd, HX * PITCH : (HX + 1) * PITCH, :] = xprev[dd].astype(jnp.bfloat16)
 
     rows1 = (H + 2) * PITCH
     row_id = lax.broadcasted_iota(jnp.int32, (rows1, LANES), 0)
@@ -352,17 +343,19 @@
         return jnp.where(hrow == 0, above, jnp.where(hrow == H + 1, below, mid))
 
     valid = jnp.where(col < WROWS, inside(0), jnp.where(col == WROWS, inside(2), inside(1)))
+    bias1 = jnp.concatenate([b1[...]] * COLS, axis=1)
+    bias2 = jnp.concatenate([b2[...]] * COLS, axis=1)
     lane_h = lax.broadcasted_iota(jnp.int32, (PITCH, LANES), 1)
 
     def layer1(d, carry):
         lhs = jnp.concatenate(
-            [x1[d + a, b * PITCH : b * PITCH + rows1, :] for a in range(3) for b in range(3)], axis=1
+            [x1[d + a, b * PITCH : b * PITCH + rows1, :] for a in range(3) for b in (1, 3)], axis=1
         )
         y = jnp.dot(lhs, w1[...], preferred_element_type=jnp.float32)
-        y = jnp.maximum(y + b1[...], 0.0)
+        y = jnp.maximum(y + bias1, 0.0)
         disp = d0 - 1 + d
-        ok = jnp.where((disp >= 0) & (disp < NDISP), 1, 0)
-        y = jnp.where(valid * ok > 0, y, 0.0)
+        least = jnp.where((disp >= 0) & (disp < NDISP), 0, 1)
+        y = jnp.where(valid > least, y, 0.0)
         for hh in range(H + 2):
             z = y[hh * PITCH : (hh + 1) * PITCH]
             zr = pltpu.roll(z, C, 1)
@@ -385,7 +378,7 @@
             [h2[d + a, b * WROWS : b * WROWS + rows2, :] for a in range(3) for b in range(3)], axis=1
         )
         y = ybuf.at[slot]
-        y[...] = jnp.dot(lhs, w2[...], preferred_element_type=jnp.float32) + b2[...]
+        y[...] = jnp.dot(lhs, w2[...], preferred_element_type=jnp.float32) + bias2
         for i in range(WROWS):
             out_ref[d, :, i * LANES : (i + 1) * LANES] = y[pl.ds(i, H, stride=WROWS), :]
 
@@ -398,15 +391,15 @@
 
 
 def group_matrix():
-    lane = np.arange(LANES)
-    source = lane[:, None] // (C // G)
-    target = np.full((LANES,), -1)
+    row = lax.broadcasted_iota(jnp.int32, (2 * LANES, LANES), 0)
+    lane = lax.broadcasted_iota(jnp.int32, (2 * LANES, LANES), 1)
+    source = lax.rem(row, LANES) // (C // G)
+    lane = lax.rem(lane, LANES // 2)
     own = COLS * G
-    target[:own] = lane[:own]
-    target[own : own + G] = lane[own - G : own]
-    target[own + G : own + 2 * G] = lane[:G]
-    mat = np.where(source == target[None, :], 1.0 / (NPV * (C // G)), 0.0)
-    return jnp.asarray(np.concatenate([mat, mat], axis=0), jnp.bfloat16)
+    target = jnp.where(
+        lane < own, lane, jnp.where(lane < own + G, lane - G, jnp.where(lane < own + 2 * G, lane - own - G, -1))
+    )
+    return jnp.where(source == target, 1.0 / (NPV * (C // G)), 0.0).astype(jnp.bfloat16)
 
 
 def on_device(
@@ -417,31 +410,33 @@
     views = lax.axis_size("views")
     nd = NDISP // views
     req = jnp.concatenate([line_owner[0, :, 0], line_index[0], line_offset[0]])
-    req = jnp.broadcast_to(jnp.pad(req, (0, LANES - req.shape[0]))[None], (8, LANES))
+    req = jnp.pad(req, (0, LANES - req.shape[0]))[None]
     body = NPV * H * LROWS + H * WROWS
-    total = -(-body // (16 * views)) * 16 * views
+    total = -(-body // (32 * views)) * 32 * views
     vmem = pl.BlockSpec(memory_space=pltpu.VMEM)
     smem = pl.BlockSpec(memory_space=pltpu.SMEM)
     hbm = pl.BlockSpec(memory_space=pl.ANY)
-    part, w1, w2 = pl.pallas_call(
+    part, w1, w2, req8 = pl.pallas_call(
         pack_kernel,
         out_shape=[
             jax.ShapeDtypeStruct((total // views, LANES), jnp.bfloat16),
-            jax.ShapeDtypeStruct((9 * LANES, LANES), jnp.bfloat16),
+            jax.ShapeDtypeStruct((6 * LANES, LANES), jnp.bfloat16),
             jax.ShapeDtypeStruct((18 * LANES, LANES), jnp.bfloat16),
+            jax.ShapeDtypeStruct((8, LANES), jnp.int32),
         ],
-        in_specs=[vmem] * 4,
-        out_specs=[vmem] * 3,
+        in_specs=[vmem] * 5,
+        out_specs=[vmem] * 4,
         scratch_shapes=[pltpu.VMEM((total, LANES), jnp.float32)],
-        compiler_params=pltpu.CompilerParams(vmem_limit_bytes=16 << 20),
+        compiler_params=pltpu.CompilerParams(vmem_limit_bytes=60 << 20),
         name="pack",
     )(
         partner_lines[0].reshape(NPV * H, SW * C),
         ref_features[0],
         conv1_weight.reshape(27 * G, CH),
         conv2_weight.reshape(27 * CH, CH),
+        req,
     )
-    hops = max(1, views.bit_length() - 1)
+    orders = hop_orders(n_tiles, views)
     dma = pltpu.SemaphoreType.DMA
     gathered, table = pl.pallas_call(
         partial(gather_kernel, n_tiles, views),
@@ -452,18 +447,20 @@
         in_specs=[hbm, hbm],
         out_specs=[hbm, hbm],
         scratch_shapes=[
-            dma((2,)), dma((n_tiles,)), dma((n_tiles,)), dma((n_tiles,)), dma((n_tiles,)),
-            dma((hops, views, n_tiles)), dma((hops, views, n_tiles)),
+            dma((len(orders),)),
+            *[dma((1 << len(order),)) for order in orders for _ in range(2)],
         ],
-        compiler_params=pltpu.CompilerParams(collective_id=0, has_side_effects=True),
+        compiler_params=pltpu.CompilerParams(
+            collective_id=0, has_side_effects=True, vmem_limit_bytes=60 << 20
+        ),
         name="gather",
-    )(part, req)
+    )(part, req8)
     nk = (nd + 4) // COLS
     f32, bf16 = jnp.float32, jnp.bfloat16
     out = pl.pallas_call(
         partial(main_kernel, nd),
         out_shape=jax.ShapeDtypeStruct((nd, H, W * CH), f32),
-        in_specs=[smem, hbm, hbm] + [vmem] * 5,
+        in_specs=[smem, hbm, hbm] + [vmem] * 4,
         out_specs=vmem,
         scratch_shapes=[
             pltpu.SMEM((n_tiles, 8, LANES), jnp.int32),
@@ -475,24 +472,24 @@
             pltpu.VMEM((COLS, 40, LANES), f32),
             pltpu.VMEM((COLS, 2, 8, LANES), f32),
             pltpu.VMEM((HX, PITCH, LANES), f32),
-            pltpu.VMEM((nk * COLS, HX * PITCH, LANES), bf16),
+            pltpu.VMEM((nk * COLS, PITCH, LANES), f32),
+            pltpu.VMEM((nk * COLS, (HX + 1) * PITCH, LANES), bf16),
             pltpu.VMEM((nd + 2, (H + 2) * WROWS, 2 * LANES), bf16),
             pltpu.VMEM((2, H * WROWS, LANES), f32),
             dma,
             dma((9,)),
             dma,
         ],
-        compiler_params=pltpu.CompilerParams(vmem_limit_bytes=48 << 20),
+        compiler_params=pltpu.CompilerParams(vmem_limit_bytes=60 << 20),
         name="volume",
     )(
-        neighbours.reshape(-1),
+        neighbours,
         table,
         gathered,
         w1,
-        jnp.tile(conv1_bias, COLS)[None],
+        conv1_bias[None],
         w2,
-        jnp.tile(conv2_bias, COLS)[None],
-        group_matrix(),
+        conv2_bias[None],
     )
     return out[None]
 

time: 92.7 us -> 66.6 us (0.72)
  the two profiles are of different devices: /device:TPU:19 before, /device:TPU:1 now
where the time goes in v2:
time: 66.6 us; the launch traced here: 66.2 us
  Pallas kernels  63.6 us (95%)
  local copies, waits for them, and re-layouts  1.87 us (3%)
  other arithmetic  0.76 us (1%)
    pallas_call x1, Pallas kernels, on_device(): pl.pallas_call(partial(gather_kernel, n_tiles, views), out_shape=[jax.Sha...  34.4 us
    pallas_call x1, Pallas kernels, on_device(): pl.pallas_call(partial(main_kernel, nd), out_shape=jax.ShapeDtypeStruct((...  25.9 us
    pallas_call x1, Pallas kernels, on_device(): pl.pallas_call(pack_kernel, out_shape=[jax.ShapeDtypeStruct((total // vie...  3.28 us
    unnamed x1, local copies, waits for them, and re-layouts  1.34 us

profile of v2, /device:TPU:1, one launch (start us, length us, event | category | flops | bytes accessed | tf_op | source)
XLA Modules:
  0.0 66.2 jit_solution(2725321444876107950)
XLA Ops:
  0.0 0.8 %pad_add_fusion = s32[96]{0:T(128)S(1)} fusion(s32[32]{0:T(128)} %bitcast.18, s32[32]{0:T(128)} %bitcast.19, s32[32]{0:T(128)} %bitcast.20), kind=kLoop, calls=%fused_computation | loop fusion | flops 192 | bytes 768 | tf_op jit(solution)/shard_map/concatenate | solution.py:412
  0.8 0.5 pad_bitcast_fusion.req_ref
  1.3 1.3 %copy.11.nb = s32[8,4]{1,0:T(8,128)} copy(s32[8,4]{0,1:T(4,128)} %param.15) | data formatting | bytes 256 | tf_op args[5]
  2.6 3.3 %pack.1 = (bf16[576,128]{1,0:T(8,128)(2,1)}, bf16[768,128]{1,0:T(8,128)(2,1)}, bf16[2304,128]{1,0:T(8,128)(2,1)}, s32[8,128]{1,0:T(8,128)}) custom-call(bf16[32,8192]{1,0:T(8,128)(2,1)} %bitcast.12, bf16[8,4096]{1,0:T(8,128)(2,1)} %bitcast.14, bf16[216,32]{1,0:T(8,128)(2,1)} %bitcast.15, bf16[864,32]{1,0:T(8,128)(2,1)} %bitcast.13, ...), custom_call_target="tpu_custom_call" | custom-call | tf_op jit(solution)/shard_map/pack/pallas_call | solution.py:419
  5.9 34.4 %gather.1 = (bf16[8,2304,128]{2,1,0:T(8,128)(2,1)}, s32[8,8,128]{2,1,0:T(8,128)}) custom-call(bf16[576,128]{1,0:T(8,128)(2,1)} %get-tuple-element.11.part_ref, s32[8,128]{1,0:T(8,128)} %get-tuple-element.12.req_ref), custom_call_target="tpu_custom_call" | custom-call | tf_op jit(solution)/shard_map/gather/pallas_call | solution.py:441
  40.3 25.9 %volume.1 = f32[16,8,4096]{2,1,0:T(8,128)} custom-call(s32[8,4]{1,0:T(8,128)} %copy.11.nb, s32[8,8,128]{2,1,0:T(8,128)} %get-tuple-element.13.tab_ref, bf16[8,2304,128]{2,1,0:T(8,128)(2,1)} %get-tuple-element.14.all_ref, bf16[768,128]{1,0:T(8,128)(2,1)} %get-tuple-element.15.w1, f32[1,32]{1,0:T(1,128)} %bitcast.16, bf16[2304,128]{1,0:T(8,128)(2,1)} %get-tuple-element.16.w2, ...), custom_call_target="tpu_custom_call" | custom-call | tf_op jit(solution)/shard_map/volume/pallas_call | solution.py:460

commit v3 on v2

--- a/solution.py
+++ b/solution.py
@@ -50,8 +50,7 @@
             out_ref[a * pitch + 3 * depth : (a + 1) * pitch, :] = jnp.zeros((pitch - 3 * depth, LANES), jnp.bfloat16)
 
 
-def pack_kernel(lines_ref, ref_ref, k1_ref, k2_ref, req_ref, out_ref, w1_ref, w2_ref, req8_ref, scr):
-    req8_ref[...] = jnp.broadcast_to(req_ref[...], req8_ref.shape)
+def pack_own(lines_ref, ref_ref, scr, part_ref):
     n_lines = lines_ref.shape[0]
     for j in range(LROWS):
         scr[pl.ds(j, n_lines, stride=LROWS), :] = lines_ref[:, j * LANES : (j + 1) * LANES].astype(jnp.float32)
@@ -61,11 +60,9 @@
     base = base + H * WROWS
     if scr.shape[0] > base:
         scr[base:, :] = jnp.zeros((scr.shape[0] - base, LANES), jnp.float32)
-    part = out_ref.shape[0]
+    part = part_ref.shape[0]
     v = lax.axis_index("views")
-    out_ref[...] = scr[pl.ds(pl.multiple_of(v * part, 16), part), :].astype(jnp.bfloat16)
-    spread_taps(k1_ref, w1_ref, LANES // 2, 2 * LANES)
-    spread_taps(k2_ref, w2_ref, 2 * LANES, 6 * LANES)
+    part_ref[...] = scr[pl.ds(pl.multiple_of(v * part, 16), part), :].astype(jnp.bfloat16)
 
 
 def hop_orders(T, V):
@@ -96,7 +93,10 @@
     return seen
 
 
-def gather_kernel(T, V, part_ref, req_ref, all_ref, tab_ref, own_sem, *sems):
+def gather_kernel(
+    T, V, lines_ref, ref_ref, owner_ref, index_ref, offset_ref, k1_ref, k2_ref,
+    all_ref, tab_ref, w1_ref, w2_ref, scr, part_ref, req_ref, own_sem, *sems
+):
     t = lax.axis_index("tiles")
     v = lax.axis_index("views")
     part = part_ref.shape[0]
@@ -117,6 +117,10 @@
     hops = orders[0]
     for hop in hops:
         pl.semaphore_signal(barrier, inc=1, device_id=across(1, [hop]), device_id_type=MESH)
+    pack_own(lines_ref, ref_ref, scr, part_ref)
+    asked = [owner_ref[...], index_ref[...], offset_ref[...]]
+    asked.append(jnp.zeros((1, LANES - 3 * asked[0].shape[1]), jnp.int32))
+    req_ref[...] = jnp.broadcast_to(jnp.concatenate(asked, axis=1), req_ref.shape)
     pl.semaphore_wait(barrier, len(hops))
 
     def place(o, mask):
@@ -150,7 +154,12 @@
 
     sent = []
     own = []
+    spread = False
     for o, mask in arrivals(orders, (1.0, 1.0, 0.02)):
+        if mask and not spread:
+            spread_taps(k1_ref, w1_ref, LANES // 2, 2 * LANES)
+            spread_taps(k2_ref, w2_ref, 2 * LANES, 6 * LANES)
+            spread = True
         if mask:
             landed(o, mask).wait_recv()
         for h in range(mask.bit_length(), len(orders[o])):
@@ -178,7 +187,7 @@
     d0 = v * nd
 
     def link(x, side):
-        got = nb[jnp.maximum(x, 0), side]
+        got = nb[side, jnp.maximum(x, 0)]
         return jnp.where(x >= 0, got, -1)
 
     mids = [t, link(t, 2), link(t, 3)]
@@ -218,11 +227,12 @@
                 index = tab[tt, 0, NPV * H + u * H + row]
                 src = pl.multiple_of((u * H + index) * LROWS, LROWS)
                 pltpu.make_async_copy(
-                    all_ref.at[owner, pl.ds(src, LROWS), :], lines.at[s * NPV + u, hh], sem_l
+                    all_ref.at[owner, pl.ds(src, LROWS), :], lines.at[hh, s * NPV + u], sem_l.at[hh]
                 ).start()
         return carry
 
-    lax.fori_loop(0, HX, fetch, 0)
+    ahead = 4
+    lax.fori_loop(0, ahead, fetch, 0)
 
     for c in copies:
         c.wait()
@@ -240,7 +250,9 @@
     linef[...] = jnp.zeros_like(linef)
     vt0[...] = jnp.zeros_like(vt0)
     vte0[...] = jnp.zeros_like(vte0)
-    pltpu.make_async_copy(lines, lines, sem_l).wait()
+
+    def arrived(hh):
+        pltpu.make_async_copy(lines.at[hh], lines.at[hh], sem_l.at[hh]).wait()
 
     lane40 = lax.broadcasted_iota(jnp.int32, (40, LANES), 1)
 
@@ -262,7 +274,7 @@
                 r0 = col - q * COLS
                 slot = s * NPV + u
                 buf = linef.at[slot]
-                buf[FRONT : FRONT + LROWS, :] = lines[slot, hh].astype(jnp.float32)
+                buf[FRONT : FRONT + LROWS, :] = lines[hh, slot].astype(jnp.float32)
                 if s == 0:
                     part = window(buf, q, 40, r0)
                 elif s == 1:
@@ -275,8 +287,6 @@
             else:
                 vte0[s - 1, hh, 0:8, :] = total
         return carry
-
-    lax.fori_loop(0, HX, assemble, 0)
 
     lane1 = lax.broadcasted_iota(jnp.int32, (1, LANES), 1)
 
@@ -327,7 +337,23 @@
                 xprev[dd] = x
         return carry
 
-    lax.fori_loop(0, HX, cost_row, 0)
+    arrived(0)
+    assemble(0, 0)
+
+    def row_fetching(hh, carry):
+        arrived(hh + 1)
+        fetch(hh + ahead, carry)
+        cost_row(hh, carry)
+        return assemble(hh + 1, carry)
+
+    def row_only(hh, carry):
+        arrived(hh + 1)
+        cost_row(hh, carry)
+        return assemble(hh + 1, carry)
+
+    lax.fori_loop(0, HX - ahead, row_fetching, 0)
+    lax.fori_loop(HX - ahead, HX - 1, row_only, 0)
+    cost_row(HX - 1, 0)
     for dd in range(nk * COLS):
         x1[dd, HX * PITCH : (HX + 1) * PITCH, :] = xprev[dd].astype(jnp.bfloat16)
 
@@ -364,13 +390,6 @@
             h2[d, hh * WROWS : (hh + 1) * WROWS, :] = both.astype(jnp.bfloat16)
         return carry
 
-    def layer1_pair(i, carry):
-        layer1(2 * i, carry)
-        layer1(2 * i + 1, carry)
-        return carry
-
-    lax.fori_loop(0, (nd + 2) // 2, layer1_pair, 0)
-
     rows2 = H * WROWS
 
     def layer2(d, slot):
@@ -382,12 +401,19 @@
         for i in range(WROWS):
             out_ref[d, :, i * LANES : (i + 1) * LANES] = y[pl.ds(i, H, stride=WROWS), :]
 
-    def layer2_pair(i, carry):
+    for d in range(4):
+        layer1(d, 0)
+
+    def both_layers(i, carry):
         layer2(2 * i, 0)
         layer2(2 * i + 1, 1)
+        layer1(2 * i + 4, carry)
+        layer1(2 * i + 5, carry)
         return carry
 
-    lax.fori_loop(0, nd // 2, layer2_pair, 0)
+    lax.fori_loop(0, nd // 2 - 1, both_layers, 0)
+    layer2(nd - 2, 0)
+    layer2(nd - 1, 1)
 
 
 def group_matrix():
@@ -409,44 +435,27 @@
     n_tiles = lax.axis_size("tiles")
     views = lax.axis_size("views")
     nd = NDISP // views
-    req = jnp.concatenate([line_owner[0, :, 0], line_index[0], line_offset[0]])
-    req = jnp.pad(req, (0, LANES - req.shape[0]))[None]
     body = NPV * H * LROWS + H * WROWS
     total = -(-body // (32 * views)) * 32 * views
     vmem = pl.BlockSpec(memory_space=pltpu.VMEM)
     smem = pl.BlockSpec(memory_space=pltpu.SMEM)
     hbm = pl.BlockSpec(memory_space=pl.ANY)
-    part, w1, w2, req8 = pl.pallas_call(
-        pack_kernel,
-        out_shape=[
-            jax.ShapeDtypeStruct((total // views, LANES), jnp.bfloat16),
-            jax.ShapeDtypeStruct((6 * LANES, LANES), jnp.bfloat16),
-            jax.ShapeDtypeStruct((18 * LANES, LANES), jnp.bfloat16),
-            jax.ShapeDtypeStruct((8, LANES), jnp.int32),
-        ],
-        in_specs=[vmem] * 5,
-        out_specs=[vmem] * 4,
-        scratch_shapes=[pltpu.VMEM((total, LANES), jnp.float32)],
-        compiler_params=pltpu.CompilerParams(vmem_limit_bytes=60 << 20),
-        name="pack",
-    )(
-        partner_lines[0].reshape(NPV * H, SW * C),
-        ref_features[0],
-        conv1_weight.reshape(27 * G, CH),
-        conv2_weight.reshape(27 * CH, CH),
-        req,
-    )
     orders = hop_orders(n_tiles, views)
     dma = pltpu.SemaphoreType.DMA
-    gathered, table = pl.pallas_call(
+    gathered, table, w1, w2 = pl.pallas_call(
         partial(gather_kernel, n_tiles, views),
         out_shape=[
             jax.ShapeDtypeStruct((n_tiles, total, LANES), jnp.bfloat16),
             jax.ShapeDtypeStruct((n_tiles, 8, LANES), jnp.int32),
+            jax.ShapeDtypeStruct((6 * LANES, LANES), jnp.bfloat16),
+            jax.ShapeDtypeStruct((18 * LANES, LANES), jnp.bfloat16),
         ],
-        in_specs=[hbm, hbm],
-        out_specs=[hbm, hbm],
+        in_specs=[vmem] * 7,
+        out_specs=[hbm, hbm, vmem, vmem],
         scratch_shapes=[
+            pltpu.VMEM((total, LANES), jnp.float32),
+            pltpu.VMEM((total // views, LANES), jnp.bfloat16),
+            pltpu.VMEM((8, LANES), jnp.int32),
             dma((len(orders),)),
             *[dma((1 << len(order),)) for order in orders for _ in range(2)],
         ],
@@ -454,7 +463,15 @@
             collective_id=0, has_side_effects=True, vmem_limit_bytes=60 << 20
         ),
         name="gather",
-    )(part, req8)
+    )(
+        partner_lines[0].reshape(NPV * H, SW * C),
+        ref_features[0],
+        line_owner.reshape(1, NPV * H),
+        line_index,
+        line_offset,
+        conv1_weight.reshape(27 * G, CH),
+        conv2_weight.reshape(27 * CH, CH),
+    )
     nk = (nd + 4) // COLS
     f32, bf16 = jnp.float32, jnp.bfloat16
     out = pl.pallas_call(
@@ -464,7 +481,7 @@
         out_specs=vmem,
         scratch_shapes=[
             pltpu.SMEM((n_tiles, 8, LANES), jnp.int32),
-            pltpu.VMEM((3 * NPV, HX, LROWS, LANES), bf16),
+            pltpu.VMEM((HX, 3 * NPV, LROWS, LANES), bf16),
             pltpu.VMEM((3, HX * WROWS, LANES), bf16),
             pltpu.VMEM((3 * NPV, LPAD, LANES), f32),
             pltpu.VMEM((HX, 48, LANES), f32),
@@ -476,14 +493,14 @@
             pltpu.VMEM((nk * COLS, (HX + 1) * PITCH, LANES), bf16),
             pltpu.VMEM((nd + 2, (H + 2) * WROWS, 2 * LANES), bf16),
             pltpu.VMEM((2, H * WROWS, LANES), f32),
-            dma,
+            dma((HX,)),
             dma((9,)),
             dma,
         ],
         compiler_params=pltpu.CompilerParams(vmem_limit_bytes=60 << 20),
         name="volume",
     )(
-        neighbours,
+        neighbours.T,
         table,
         gathered,
         w1,

time: 66.6 us -> 58.5 us (0.88)
  Pallas kernels: 63.6 us -> 58.3 us
  local copies, waits for them, and re-layouts: 1.87 us -> 0 us
  other arithmetic: 0.76 us -> 0 us
    pallas_call x1, Pallas kernels: 25.9 us -> 21.8 us  [on_device(): pl.pallas_call(partial(main_kernel, nd), out_shape=jax.ShapeDtypeStruct((...]
    pallas_call x1 -> x0, Pallas kernels: 3.28 us -> none  [on_device(): pl.pallas_call(pack_kernel, out_shape=[jax.ShapeDtypeStruct((total // vie...]
    pallas_call x1, Pallas kernels: 34.4 us -> 36.5 us  [on_device(): pl.pallas_call(partial(gather_kernel, n_tiles, views), out_shape=[jax.Sha...]
    unnamed x1 -> x0, local copies, waits for them, and re-layouts: 1.34 us -> none
    concatenate x1 -> x0, other arithmetic: 0.76 us -> none  [on_device(): req = jnp.concatenate([line_owner[0, :, 0], line_index[0], line_offset[0]])]
where the time goes in v3:
time: 58.5 us; the launch traced here: 58.3 us
  Pallas kernels  58.3 us (100%)
    pallas_call x1, Pallas kernels, on_device(): pl.pallas_call(partial(gather_kernel, n_tiles, views), out_shape=[jax.Sha...  36.5 us
    pallas_call x1, Pallas kernels, on_device(): pl.pallas_call(partial(main_kernel, nd), out_shape=jax.ShapeDtypeStruct((...  21.8 us

profile of v3, /device:TPU:1, one launch (start us, length us, event | category | flops | bytes accessed | tf_op | source)
XLA Modules:
  0.0 58.3 jit_solution(13415846980710057692)
XLA Ops:
  0.0 36.5 %gather.1 = (bf16[8,2304,128]{2,1,0:T(8,128)(2,1)}, s32[8,8,128]{2,1,0:T(8,128)}, bf16[768,128]{1,0:T(8,128)(2,1)}, bf16[2304,128]{1,0:T(8,128)(2,1)}) custom-call(bf16[32,8192]{1,0:T(8,128)(2,1)} %bitcast.9, bf16[8,4096]{1,0:T(8,128)(2,1)} %bitcast.11, s32[1,32]{1,0:T(1,128)} %bitcast.14, s32[1,32]{1,0:T(1,128)} %index_ref.1, s32[1,32]{1,0:T(1,128)} %offset_ref.1, ...), custom_call_target="tpu_custom_call" | custom-call | tf_op jit(solution)/shard_map/gather/pallas_call | solution.py:445
  36.5 21.8 %volume.1 = f32[16,8,4096]{2,1,0:T(8,128)} custom-call(s32[4,8]{1,0:T(4,128)} %bitcast.13, s32[8,8,128]{2,1,0:T(8,128)} %get-tuple-element.9.tab_ref, bf16[8,2304,128]{2,1,0:T(8,128)(2,1)} %get-tuple-element.10.all_ref, bf16[768,128]{1,0:T(8,128)(2,1)} %get-tuple-element.11.w1, f32[1,32]{1,0:T(1,128)} %bitcast.15, bf16[2304,128]{1,0:T(8,128)(2,1)} %get-tuple-element.12.w2, ...), custom_call_target="tpu_custom_call" | custom-call | tf_op jit(solution)/shard_map/volume/pallas_call | solution.py:477

commit v4 on v3

--- a/solution.py
+++ b/solution.py
@@ -60,9 +60,7 @@
     base = base + H * WROWS
     if scr.shape[0] > base:
         scr[base:, :] = jnp.zeros((scr.shape[0] - base, LANES), jnp.float32)
-    part = part_ref.shape[0]
-    v = lax.axis_index("views")
-    part_ref[...] = scr[pl.ds(pl.multiple_of(v * part, 16), part), :].astype(jnp.bfloat16)
+    part_ref[...] = scr[...].astype(jnp.bfloat16)
 
 
 def hop_orders(T, V):
@@ -76,21 +74,46 @@
     tb, vb = bits(0, T), bits(1, V)
     first = tb + vb
     second = tb[:-1] + vb[:1] + tb[-1:] + vb[1:]
-    return first, second, tb
+    third = tb[:1] + tb[-1:] + vb[:1] + tb[1:-1] + vb[1:]
+    return first, second, third, tb
+
+
+def split_rows(part):
+    units = part // 16
+    third = units // 4
+    second = (units - third) * 2 // 5
+    return [(units - second - third) * 16, second * 16, third * 16]
+
+
+def own_masks(order):
+    views = [1 << h for h, (axis, _) in enumerate(order) if axis == 1]
+    masks = [0]
+    for bit in views:
+        masks = masks + [mask | bit for mask in masks]
+    return masks
 
 
 def arrivals(orders, costs):
     free = {}
-    heap = [(0.0, o, 0) for o in range(len(orders))]
+    heap = []
+    for o, order in enumerate(orders):
+        for mask in own_masks(order):
+            heapq.heappush(heap, (0.0, o, mask))
     seen = []
     while heap:
         now, o, mask = heapq.heappop(heap)
         seen.append((o, mask))
-        for h in range(mask.bit_length(), len(orders[o])):
-            hop = orders[o][h]
-            free[hop] = max(free.get(hop, 0.0), now) + costs[o] * (0.2 if hop == (1, 1) else 1.0)
-            heapq.heappush(heap, (free[hop], o, mask | (1 << h)))
+        for h in onward(orders[o], mask):
+            axis, bit = orders[o][h]
+            link = (axis, min(bit, 2))
+            free[link] = max(free.get(link, 0.0), now) + costs[o] * (0.2 if link == (1, 1) else 1.0)
+            heapq.heappush(heap, (free[link] + 0.5, o, mask | (1 << h)))
     return seen
+
+
+def onward(order, mask):
+    own = own_masks(order)
+    return [h for h in range(mask.bit_length(), len(order)) if mask | (1 << h) not in own]
 
 
 def gather_kernel(
@@ -99,9 +122,11 @@
 ):
     t = lax.axis_index("tiles")
     v = lax.axis_index("views")
-    part = part_ref.shape[0]
-    half = part // 2
+    part = part_ref.shape[0] // V
     orders = hop_orders(T, V)
+    counts = split_rows(part)
+    starts = [sum(counts[:o]) for o in range(len(counts))]
+    last = len(orders) - 1
 
     def flip(x, bit):
         return x + bit - 2 * bit * lax.rem(lax.div(x, bit), 2)
@@ -125,16 +150,21 @@
 
     def place(o, mask):
         tile, view = across(mask, orders[o])
-        if o == 2:
+        if o == last:
             return tab_ref.at[tile]
-        return all_ref.at[tile, pl.ds(pl.multiple_of(view * part + o * half, 16), half), :]
-
-    def source(o):
-        return req_ref if o == 2 else part_ref.at[pl.ds(o * half, half), :]
+        return all_ref.at[tile, pl.ds(pl.multiple_of(view * part + starts[o], 16), counts[o]), :]
+
+    def source(o, mask):
+        if mask not in own_masks(orders[o]):
+            return place(o, mask)
+        if o == last:
+            return req_ref
+        view = across(mask, orders[o])[1]
+        return part_ref.at[pl.ds(pl.multiple_of(view * part + starts[o], 16), counts[o]), :]
 
     def send(o, mask, h):
         return pltpu.make_async_remote_copy(
-            src_ref=source(o) if mask == 0 else place(o, mask),
+            src_ref=source(o, mask),
             dst_ref=place(o, mask),
             send_sem=sems[2 * o].at[mask | (1 << h)],
             recv_sem=sems[2 * o + 1].at[mask | (1 << h)],
@@ -152,24 +182,25 @@
             device_id_type=MESH,
         )
 
+    own = [
+        pltpu.make_async_copy(part_ref, all_ref.at[t], own_sem.at[0]),
+        pltpu.make_async_copy(req_ref, tab_ref.at[t], own_sem.at[1]),
+    ]
     sent = []
-    own = []
-    spread = False
-    for o, mask in arrivals(orders, (1.0, 1.0, 0.02)):
-        if mask and not spread:
+    scale = 1.0 / part
+    landing = arrivals(orders, [count * scale for count in counts] + [0.01])
+    for n, (o, mask) in enumerate(landing):
+        if n == len(landing) // 2:
+            for copy in own:
+                copy.start()
             spread_taps(k1_ref, w1_ref, LANES // 2, 2 * LANES)
             spread_taps(k2_ref, w2_ref, 2 * LANES, 6 * LANES)
-            spread = True
-        if mask:
+        if mask not in own_masks(orders[o]):
             landed(o, mask).wait_recv()
-        for h in range(mask.bit_length(), len(orders[o])):
+        for h in onward(orders[o], mask):
             copy = send(o, mask, h)
             copy.start()
             sent.append(copy)
-        if mask == 0:
-            mine = pltpu.make_async_copy(source(o), place(o, 0), own_sem.at[o])
-            mine.start()
-            own.append(mine)
     for copy in own:
         copy.wait()
     for copy in sent:
@@ -177,11 +208,15 @@
 
 
 def main_kernel(
-    nd, nb, tab_ref, all_ref, w1, b1, w2, b2, out_ref,
-    tab, lines, refb, linef, vt0, vte0, vt, vte, refx, xprev, x1, h2, ybuf, sem_l, sem_r, sem_t,
+    nd, nb, tab_ref, all_ref, w1_ref, b1, w2_ref, b2, out_ref,
+    w1, w2, obuf, tab, lines, refb, linef, vt0, vte0, vt, vte, refx, xprev, x1, h2, ybuf, sem_l, sem_r, sem_t, sem_w, sem_o,
 ):
     table_copy = pltpu.make_async_copy(tab_ref, tab, sem_t)
     table_copy.start()
+    weights = [
+        pltpu.make_async_copy(w1_ref, w1, sem_w.at[0]),
+        pltpu.make_async_copy(w2_ref, w2, sem_w.at[1]),
+    ]
     t = lax.axis_index("tiles")
     v = lax.axis_index("views")
     d0 = v * nd
@@ -233,6 +268,8 @@
 
     ahead = 4
     lax.fori_loop(0, ahead, fetch, 0)
+    for copy in weights:
+        copy.start()
 
     for c in copies:
         c.wait()
@@ -392,6 +429,9 @@
 
     rows2 = H * WROWS
 
+    def slab_out(d):
+        return pltpu.make_async_copy(obuf.at[d], out_ref.at[d], sem_o.at[d])
+
     def layer2(d, slot):
         lhs = jnp.concatenate(
             [h2[d + a, b * WROWS : b * WROWS + rows2, :] for a in range(3) for b in range(3)], axis=1
@@ -399,8 +439,11 @@
         y = ybuf.at[slot]
         y[...] = jnp.dot(lhs, w2[...], preferred_element_type=jnp.float32) + bias2
         for i in range(WROWS):
-            out_ref[d, :, i * LANES : (i + 1) * LANES] = y[pl.ds(i, H, stride=WROWS), :]
-
+            obuf[d, :, i * LANES : (i + 1) * LANES] = y[pl.ds(i, H, stride=WROWS), :]
+        slab_out(d).start()
+
+    for copy in weights:
+        copy.wait()
     for d in range(4):
         layer1(d, 0)
 
@@ -414,6 +457,12 @@
     lax.fori_loop(0, nd // 2 - 1, both_layers, 0)
     layer2(nd - 2, 0)
     layer2(nd - 1, 1)
+
+    def slab_done(d, carry):
+        slab_out(d).wait()
+        return carry
+
+    lax.fori_loop(0, nd, slab_done, 0)
 
 
 def group_matrix():
@@ -436,7 +485,7 @@
     views = lax.axis_size("views")
     nd = NDISP // views
     body = NPV * H * LROWS + H * WROWS
-    total = -(-body // (32 * views)) * 32 * views
+    total = -(-body // (16 * views)) * 16 * views
     vmem = pl.BlockSpec(memory_space=pltpu.VMEM)
     smem = pl.BlockSpec(memory_space=pltpu.SMEM)
     hbm = pl.BlockSpec(memory_space=pl.ANY)
@@ -454,9 +503,9 @@
         out_specs=[hbm, hbm, vmem, vmem],
         scratch_shapes=[
             pltpu.VMEM((total, LANES), jnp.float32),
-            pltpu.VMEM((total // views, LANES), jnp.bfloat16),
+            pltpu.VMEM((total, LANES), jnp.bfloat16),
             pltpu.VMEM((8, LANES), jnp.int32),
-            dma((len(orders),)),
+            dma((2,)),
             *[dma((1 << len(order),)) for order in orders for _ in range(2)],
         ],
         compiler_params=pltpu.CompilerParams(
@@ -477,9 +526,12 @@
     out = pl.pallas_call(
         partial(main_kernel, nd),
         out_shape=jax.ShapeDtypeStruct((nd, H, W * CH), f32),
-        in_specs=[smem, hbm, hbm] + [vmem] * 4,
-        out_specs=vmem,
+        in_specs=[smem, hbm, hbm, hbm, vmem, hbm, vmem],
+        out_specs=hbm,
         scratch_shapes=[
+            pltpu.VMEM((6 * LANES, LANES), bf16),
+            pltpu.VMEM((18 * LANES, LANES), bf16),
+            pltpu.VMEM((nd, H, W * CH), f32),
             pltpu.SMEM((n_tiles, 8, LANES), jnp.int32),
             pltpu.VMEM((HX, 3 * NPV, LROWS, LANES), bf16),
             pltpu.VMEM((3, HX * WROWS, LANES), bf16),
@@ -496,6 +548,8 @@
             dma((HX,)),
             dma((9,)),
             dma,
+            dma((2,)),
+            dma((nd,)),
         ],
         compiler_params=pltpu.CompilerParams(vmem_limit_bytes=60 << 20),
         name="volume",

time: 58.5 us -> 56.3 us (0.962)
  Pallas kernels: 58.3 us -> 56 us
    pallas_call x1, Pallas kernels: 36.5 us -> 35.1 us  [on_device(): pl.pallas_call(partial(gather_kernel, n_tiles, views), out_shape=[jax.Sha...]
    pallas_call x1, Pallas kernels: 21.8 us -> 20.9 us  [on_device(): pl.pallas_call(partial(main_kernel, nd), out_shape=jax.ShapeDtypeStruct((...]
where the time goes in v4:
time: 56.3 us; the launch traced here: 56 us
  Pallas kernels  56 us (99%)
    pallas_call x1, Pallas kernels, on_device(): pl.pallas_call(partial(gather_kernel, n_tiles, views), out_shape=[jax.Sha...  35.1 us
    pallas_call x1, Pallas kernels, on_device(): pl.pallas_call(partial(main_kernel, nd), out_shape=jax.ShapeDtypeStruct((...  20.9 us

profile of v4, /device:TPU:1, one launch (start us, length us, event | category | flops | bytes accessed | tf_op | source)
XLA Modules:
  0.0 56.0 jit_solution(11072895000770602713)
XLA Ops:
  0.0 35.1 %gather.1 = (bf16[8,2304,128]{2,1,0:T(8,128)(2,1)}, s32[8,8,128]{2,1,0:T(8,128)}, bf16[768,128]{1,0:T(8,128)(2,1)}, bf16[2304,128]{1,0:T(8,128)(2,1)}) custom-call(bf16[32,8192]{1,0:T(8,128)(2,1)} %bitcast.9, bf16[8,4096]{1,0:T(8,128)(2,1)} %bitcast.11, s32[1,32]{1,0:T(1,128)} %bitcast.14, s32[1,32]{1,0:T(1,128)} %index_ref.1, s32[1,32]{1,0:T(1,128)} %offset_ref.1, ...), custom_call_target="tpu_custom_call" | custom-call | tf_op jit(solution)/shard_map/gather/pallas_call | solution.py:494
  35.1 20.9 %volume.1 = f32[16,8,4096]{2,1,0:T(8,128)} custom-call(s32[4,8]{1,0:T(4,128)} %bitcast.13, s32[8,8,128]{2,1,0:T(8,128)} %get-tuple-element.9.tab_ref, bf16[8,2304,128]{2,1,0:T(8,128)(2,1)} %get-tuple-element.10.all_ref, bf16[768,128]{1,0:T(8,128)(2,1)} %get-tuple-element.11.w1_ref, f32[1,32]{1,0:T(1,128)} %bitcast.15, ...), custom_call_target="tpu_custom_call" | custom-call | tf_op jit(solution)/shard_map/volume/pallas_call | solution.py:526

commit v5 on v4

--- a/solution.py
+++ b/solution.py
@@ -213,10 +213,16 @@
 ):
     table_copy = pltpu.make_async_copy(tab_ref, tab, sem_t)
     table_copy.start()
-    weights = [
-        pltpu.make_async_copy(w1_ref, w1, sem_w.at[0]),
-        pltpu.make_async_copy(w2_ref, w2, sem_w.at[1]),
-    ]
+    weights = []
+    for n, (src, dst) in enumerate(((w1_ref, w1), (w2_ref, w2))):
+        depth = src.shape[0]
+        tap = depth // 3
+        weights.append(pltpu.make_async_copy(src, dst.at[0:depth, 0:LANES], sem_w.at[2 * n]))
+        weights.append(
+            pltpu.make_async_copy(src, dst.at[tap : tap + depth, LANES : 2 * LANES], sem_w.at[2 * n + 1])
+        )
+        dst[depth:, 0:LANES] = jnp.zeros((tap, LANES), jnp.bfloat16)
+        dst[0:tap, LANES : 2 * LANES] = jnp.zeros((tap, LANES), jnp.bfloat16)
     t = lax.axis_index("tiles")
     v = lax.axis_index("views")
     d0 = v * nd
@@ -410,53 +416,52 @@
     bias2 = jnp.concatenate([b2[...]] * COLS, axis=1)
     lane_h = lax.broadcasted_iota(jnp.int32, (PITCH, LANES), 1)
 
-    def layer1(d, carry):
+    def layer1(d):
         lhs = jnp.concatenate(
-            [x1[d + a, b * PITCH : b * PITCH + rows1, :] for a in range(3) for b in (1, 3)], axis=1
+            [x1[d + a, b * PITCH : b * PITCH + rows1, :] for a in range(4) for b in (1, 3)], axis=1
         )
-        y = jnp.dot(lhs, w1[...], preferred_element_type=jnp.float32)
-        y = jnp.maximum(y + bias1, 0.0)
-        disp = d0 - 1 + d
-        least = jnp.where((disp >= 0) & (disp < NDISP), 0, 1)
-        y = jnp.where(valid > least, y, 0.0)
-        for hh in range(H + 2):
-            z = y[hh * PITCH : (hh + 1) * PITCH]
-            zr = pltpu.roll(z, C, 1)
-            extra = jnp.where(lane_h < CH, pltpu.roll(zr, 1, 0), pltpu.roll(zr, PITCH - 1, 0))
-            both = jnp.concatenate([z[:WROWS], extra[:WROWS]], axis=1)
-            h2[d, hh * WROWS : (hh + 1) * WROWS, :] = both.astype(jnp.bfloat16)
-        return carry
+        pair = jnp.dot(lhs, w1[...], preferred_element_type=jnp.float32)
+        for j in range(2):
+            y = jnp.maximum(pair[:, j * LANES : (j + 1) * LANES] + bias1, 0.0)
+            disp = d0 - 1 + d + j
+            least = jnp.where((disp >= 0) & (disp < NDISP), 0, 1)
+            y = jnp.where(valid > least, y, 0.0)
+            for hh in range(H + 2):
+                z = y[hh * PITCH : (hh + 1) * PITCH]
+                zr = pltpu.roll(z, C, 1)
+                extra = jnp.where(lane_h < CH, pltpu.roll(zr, 1, 0), pltpu.roll(zr, PITCH - 1, 0))
+                both = jnp.concatenate([z[:WROWS], extra[:WROWS]], axis=1)
+                h2[d + j, hh * WROWS : (hh + 1) * WROWS, :] = both.astype(jnp.bfloat16)
 
     rows2 = H * WROWS
 
     def slab_out(d):
         return pltpu.make_async_copy(obuf.at[d], out_ref.at[d], sem_o.at[d])
 
-    def layer2(d, slot):
+    def layer2(d):
         lhs = jnp.concatenate(
-            [h2[d + a, b * WROWS : b * WROWS + rows2, :] for a in range(3) for b in range(3)], axis=1
+            [h2[d + a, b * WROWS : b * WROWS + rows2, :] for a in range(4) for b in range(3)], axis=1
         )
-        y = ybuf.at[slot]
-        y[...] = jnp.dot(lhs, w2[...], preferred_element_type=jnp.float32) + bias2
-        for i in range(WROWS):
-            obuf[d, :, i * LANES : (i + 1) * LANES] = y[pl.ds(i, H, stride=WROWS), :]
-        slab_out(d).start()
+        pair = jnp.dot(lhs, w2[...], preferred_element_type=jnp.float32)
+        for j in range(2):
+            y = ybuf.at[j]
+            y[...] = pair[:, j * LANES : (j + 1) * LANES] + bias2
+            for i in range(WROWS):
+                obuf[d + j, :, i * LANES : (i + 1) * LANES] = y[pl.ds(i, H, stride=WROWS), :]
+            slab_out(d + j).start()
 
     for copy in weights:
         copy.wait()
-    for d in range(4):
-        layer1(d, 0)
+    layer1(0)
+    layer1(2)
 
     def both_layers(i, carry):
-        layer2(2 * i, 0)
-        layer2(2 * i + 1, 1)
-        layer1(2 * i + 4, carry)
-        layer1(2 * i + 5, carry)
+        layer2(2 * i)
+        layer1(2 * i + 4)
         return carry
 
     lax.fori_loop(0, nd // 2 - 1, both_layers, 0)
-    layer2(nd - 2, 0)
-    layer2(nd - 1, 1)
+    layer2(nd - 2)
 
     def slab_done(d, carry):
         slab_out(d).wait()
@@ -529,8 +534,8 @@
         in_specs=[smem, hbm, hbm, hbm, vmem, hbm, vmem],
         out_specs=hbm,
         scratch_shapes=[
-            pltpu.VMEM((6 * LANES, LANES), bf16),
-            pltpu.VMEM((18 * LANES, LANES), bf16),
+            pltpu.VMEM((8 * LANES, 2 * LANES), bf16),
+            pltpu.VMEM((24 * LANES, 2 * LANES), bf16),
             pltpu.VMEM((nd, H, W * CH), f32),
             pltpu.SMEM((n_tiles, 8, LANES), jnp.int32),
             pltpu.VMEM((HX, 3 * NPV, LROWS, LANES), bf16),
@@ -548,7 +553,7 @@
             dma((HX,)),
             dma((9,)),
             dma,
-            dma((2,)),
+            dma((4,)),
             dma((nd,)),
         ],
         compiler_params=pltpu.CompilerParams(vmem_limit_bytes=60 << 20),

time: 56.3 us -> 54.5 us (0.968)
  Pallas kernels: 56 us -> 54.3 us
    pallas_call x1, Pallas kernels: 20.9 us -> 19.2 us  [on_device(): pl.pallas_call(partial(main_kernel, nd), out_shape=jax.ShapeDtypeStruct((...]
where the time goes in v5:
time: 54.5 us; the launch traced here: 54.3 us
  Pallas kernels  54.3 us (100%)
    pallas_call x1, Pallas kernels, on_device(): pl.pallas_call(partial(gather_kernel, n_tiles, views), out_shape=[jax.Sha...  35.1 us
    pallas_call x1, Pallas kernels, on_device(): pl.pallas_call(partial(main_kernel, nd), out_shape=jax.ShapeDtypeStruct((...  19.2 us

profile of v5, /device:TPU:1, one launch (start us, length us, event | category | flops | bytes accessed | tf_op | source)
XLA Modules:
  0.0 54.3 jit_solution(10666019738055253973)
XLA Ops:
  0.0 35.1 %gather.1 = (bf16[8,2304,128]{2,1,0:T(8,128)(2,1)}, s32[8,8,128]{2,1,0:T(8,128)}, bf16[768,128]{1,0:T(8,128)(2,1)}, bf16[2304,128]{1,0:T(8,128)(2,1)}) custom-call(bf16[32,8192]{1,0:T(8,128)(2,1)} %bitcast.9, bf16[8,4096]{1,0:T(8,128)(2,1)} %bitcast.11, s32[1,32]{1,0:T(1,128)} %bitcast.14, s32[1,32]{1,0:T(1,128)} %index_ref.1, s32[1,32]{1,0:T(1,128)} %offset_ref.1, ...), custom_call_target="tpu_custom_call" | custom-call | tf_op jit(solution)/shard_map/gather/pallas_call | solution.py:499
  35.1 19.2 %volume.1 = f32[16,8,4096]{2,1,0:T(8,128)} custom-call(s32[4,8]{1,0:T(4,128)} %bitcast.13, s32[8,8,128]{2,1,0:T(8,128)} %get-tuple-element.9.tab_ref, bf16[8,2304,128]{2,1,0:T(8,128)(2,1)} %get-tuple-element.10.all_ref, bf16[768,128]{1,0:T(8,128)(2,1)} %get-tuple-element.11.w1_ref, f32[1,32]{1,0:T(1,128)} %bitcast.15, ...), custom_call_target="tpu_custom_call" | custom-call | tf_op jit(solution)/shard_map/volume/pallas_call | solution.py:531
